TPU v7x, 32 devices: a whole 2x2x4 slice. The times are simulated.
32 devices in a mesh: batch: 8 (over z, x), head: 4 (over y, core).
Axes of the slice: x: 2, y: 2, z: 4, core: 2. Of those that a mesh axis runs over, the one named last changes fastest.
Arguments:
- tokens: bfloat16 [8192, 768], P('batch'), may hold values from -6 to 6
- lengths: int32 [16], P('batch'), may hold values from 64 to 512, as said below
- w_query: bfloat16 [768, 768], P(None, 'head'), may hold values from -0.21875 to 0.21875
- w_key: bfloat16 [768, 768], P(None, 'head'), may hold values from -0.21875 to 0.21875
- w_value: bfloat16 [768, 768], P(None, 'head'), may hold values from -0.21875 to 0.21875
- w_out: bfloat16 [768, 768], P('head'), may hold values from -1.75 to 1.75
- query_down_frozen: bfloat16 [768, 8], replicated, may hold values from -0.21875 to 0.21875
- value_down_frozen: bfloat16 [768, 8], replicated, may hold values from -0.21875 to 0.21875
- query_up_trained: bfloat16 [8, 768], P(None, 'head'), may hold values from -1 to 1
- value_up_trained: bfloat16 [8, 768], P(None, 'head'), may hold values from -1 to 1
- w_up: bfloat16 [768, 3072], P(None, 'head'), may hold values from -0.21875 to 0.21875
- w_down: bfloat16 [3072, 768], P('head'), may hold values from -0.109375 to 0.109375
- gain_attn: float32 [768], replicated, may hold values from 0.1 to 1.9
- gain_ffn: float32 [768], replicated, may hold values from 0.1 to 1.9
- cotangent: bfloat16 [8192, 768], P('batch'), may hold values from -6 to 6
Outputs:
- activations: bfloat16 [8192, 768], P('batch')
- input_grad: bfloat16 [8192, 768], P('batch')
- grad_b_query: float32 [8, 768], P(None, 'head')
- grad_b_value: float32 [8, 768], P(None, 'head')
Inputs may be any that keep to these rules, and one draw needn't show every extreme that they name: `lengths`: some sequence has all 512 tokens in every draw.
All inputs are finite; a program needn't handle non-finite values.
Results may differ from a plain program's by a relative error of at most 0.018.
The roundings to bfloat16 on the way count: a program that leaves them out, or rounds other values in their place, can miss the bound.
Values may be sent and summed in bfloat16 or wider, within the bound.
A program may use at most 64 MiB of HBM per device.

v0:
```python
import jax
import jax.numpy as jnp
from jax import lax
from jax.sharding import PartitionSpec as P

HD = 64


def norm_fwd(value_in, gain_vec):
    centre = value_in - jnp.mean(value_in, axis=-1, keepdims=True)
    inv_std = lax.rsqrt(jnp.mean(centre * centre, axis=-1, keepdims=True) + 1e-05)
    normed = centre * inv_std
    return (normed * gain_vec, normed, inv_std)


def norm_back(grad_in, normed, inv_std, gain_vec):
    scaled = grad_in * gain_vec
    return inv_std * (
        scaled
        - jnp.mean(scaled, axis=-1, keepdims=True)
        - normed * jnp.mean(scaled * normed, axis=-1, keepdims=True)
    )


def split_heads(matrix):
    return matrix.reshape(matrix.shape[0], matrix.shape[1] // HD, HD)


def mask_scores(query_heads, key_heads, length):
    scores = (
        jnp.einsum("qhd,khd->hqk", query_heads, key_heads, preferred_element_type=jnp.float32)
        * 0.125
    )
    key_keep = jnp.arange(key_heads.shape[0], dtype=jnp.int32) < length
    return jnp.where(key_keep[None, None, :], scores, -1e30)


def attend(packed):
    queries, key_rows, values, length = packed
    query_heads, key_heads, value_heads = (
        split_heads(queries),
        split_heads(key_rows),
        split_heads(values),
    )
    scores = mask_scores(query_heads, key_heads, length)
    row_top = jnp.max(scores, axis=-1, keepdims=True)
    exponent = jnp.exp(scores - row_top)
    totals = jnp.sum(exponent, axis=-1, keepdims=True)
    probability = exponent / totals
    logsum = row_top + jnp.log(totals)
    context = jnp.einsum(
        "hqk,khd->qhd",
        probability.astype(jnp.bfloat16),
        value_heads,
        preferred_element_type=jnp.float32,
    )
    return (context.reshape(queries.shape).astype(jnp.bfloat16), logsum)


def attend_back(packed):
    queries, key_rows, values, grad_context, logsum, length = packed
    query_heads, key_heads, value_heads = (
        split_heads(queries),
        split_heads(key_rows),
        split_heads(values),
    )
    ctx_heads = split_heads(grad_context)
    probability = jnp.exp(mask_scores(query_heads, key_heads, length) - logsum)
    grad_weights = jnp.einsum(
        "qhd,khd->hqk", ctx_heads, value_heads, preferred_element_type=jnp.float32
    )
    grad_values = jnp.einsum(
        "hqk,qhd->khd",
        probability.astype(jnp.bfloat16),
        ctx_heads,
        preferred_element_type=jnp.float32,
    )
    grad_scores = (
        probability * (grad_weights - jnp.sum(probability * grad_weights, axis=-1, keepdims=True))
    ).astype(jnp.bfloat16)
    grad_queries = 0.125 * jnp.einsum(
        "hqk,khd->qhd", grad_scores, key_heads, preferred_element_type=jnp.float32
    )
    grad_keys = 0.125 * jnp.einsum(
        "hqk,qhd->khd", grad_scores, query_heads, preferred_element_type=jnp.float32
    )
    shape_out = queries.shape
    return (
        grad_queries.reshape(shape_out).astype(jnp.bfloat16),
        grad_keys.reshape(shape_out).astype(jnp.bfloat16),
        grad_values.reshape(shape_out).astype(jnp.bfloat16),
    )


def body(
    tokens,
    lengths,
    w_query,
    w_key,
    w_value,
    w_out,
    query_down_frozen,
    value_down_frozen,
    query_up_trained,
    value_up_trained,
    w_up,
    w_down,
    gain_attn,
    gain_ffn,
    cotangent,
):
    single_float = jnp.float32
    bf16 = jnp.bfloat16
    row_count = tokens.shape[0]
    seq_count = lengths.shape[0]
    seq_span = row_count // seq_count
    local_width = w_query.shape[1]
    valid = (
        (jnp.arange(seq_span, dtype=jnp.int32)[None, :] < lengths[:, None])
        .astype(single_float)
        .reshape(row_count, 1)
    )
    low_query = jnp.dot(tokens, query_down_frozen, preferred_element_type=single_float).astype(bf16)
    low_value = jnp.dot(tokens, value_down_frozen, preferred_element_type=single_float).astype(bf16)
    queries = (
        jnp.dot(tokens, w_query, preferred_element_type=single_float)
        + 2.0 * jnp.dot(low_query, query_up_trained, preferred_element_type=single_float)
    ).astype(bf16)
    key_rows = jnp.dot(tokens, w_key, preferred_element_type=single_float).astype(bf16)
    values = (
        jnp.dot(tokens, w_value, preferred_element_type=single_float)
        + 2.0 * jnp.dot(low_value, value_up_trained, preferred_element_type=single_float)
    ).astype(bf16)
    seq_shape = (seq_count, seq_span, local_width)
    query_seq, key_seq, value_seq = (
        queries.reshape(seq_shape),
        key_rows.reshape(seq_shape),
        values.reshape(seq_shape),
    )
    context, logsum = lax.map(attend, (query_seq, key_seq, value_seq, lengths))
    context = context.reshape(row_count, local_width)
    attn_part = jnp.dot(context, w_out, preferred_element_type=single_float)
    out_grad = cotangent.astype(single_float) * valid
    attn = lax.psum(attn_part, "head")
    hidden_one, normed_one, inv_one = norm_fwd(tokens.astype(single_float) + attn, gain_attn)
    hidden_low = hidden_one.astype(bf16)
    up_pre = jnp.dot(hidden_low, w_up, preferred_element_type=single_float)
    act = jax.nn.gelu(up_pre, approximate=False).astype(bf16)
    ffn_part = jnp.dot(act, w_down, preferred_element_type=single_float)
    ffn_total = lax.psum(ffn_part, "head")
    out_full, normed_two, inv_two = norm_fwd(hidden_one + ffn_total, gain_ffn)
    activations = (valid * out_full).astype(bf16)
    grad_z2 = norm_back(out_grad, normed_two, inv_two, gain_ffn)
    grad_z2_low = grad_z2.astype(bf16)
    grad_act = jnp.dot(grad_z2_low, w_down.T, preferred_element_type=single_float)
    pre_again = jnp.dot(hidden_low, w_up, preferred_element_type=single_float)
    gelu_out, gelu_pull = jax.vjp(lambda inner: jax.nn.gelu(inner, approximate=False), pre_again)
    grad_up = gelu_pull(grad_act)[0].astype(bf16)
    hidden_part = jnp.dot(grad_up, w_up.T, preferred_element_type=single_float)
    grad_h1 = grad_z2 + lax.psum(hidden_part, "head")
    grad_z1 = norm_back(grad_h1, normed_one, inv_one, gain_attn)
    grad_z1_low = grad_z1.astype(bf16)
    grad_context = jnp.dot(grad_z1_low, w_out.T, preferred_element_type=single_float).astype(bf16)
    query_gradient, grad_k, value_gradient = lax.map(
        attend_back,
        (query_seq, key_seq, value_seq, grad_context.reshape(seq_shape), logsum, lengths),
    )
    query_gradient = query_gradient.reshape(row_count, local_width)
    grad_k = grad_k.reshape(row_count, local_width)
    value_gradient = value_gradient.reshape(row_count, local_width)
    adapter_query_gradient = 2.0 * jnp.dot(
        query_gradient, query_up_trained.T, preferred_element_type=single_float
    )
    adapter_value_gradient = 2.0 * jnp.dot(
        value_gradient, value_up_trained.T, preferred_element_type=single_float
    )
    input_part = jnp.dot(query_gradient, w_query.T, preferred_element_type=single_float)
    input_part = input_part + jnp.dot(grad_k, w_key.T, preferred_element_type=single_float)
    input_part = input_part + jnp.dot(
        value_gradient, w_value.T, preferred_element_type=single_float
    )
    input_part = input_part + jnp.dot(
        adapter_query_gradient,
        query_down_frozen.astype(single_float).T,
        precision=lax.Precision.HIGHEST,
    )
    input_part = input_part + jnp.dot(
        adapter_value_gradient,
        value_down_frozen.astype(single_float).T,
        precision=lax.Precision.HIGHEST,
    )
    input_grad = (
        grad_z1 + lax.psum(input_part.astype(jnp.bfloat16), "head").astype(jnp.float32)
    ).astype(bf16)
    query_term = 2.0 * jnp.dot(low_query.T, query_gradient, preferred_element_type=single_float)
    value_term = 2.0 * jnp.dot(low_value.T, value_gradient, preferred_element_type=single_float)
    grad_b_query, grad_b_value = lax.psum((query_term, value_term), "batch")
    return (activations, input_grad, grad_b_query, grad_b_value)


def solution(mesh):
    in_specs = (
        P("batch", None),
        P("batch"),
        P(None, "head"),
        P(None, "head"),
        P(None, "head"),
        P("head", None),
        P(),
        P(),
        P(None, "head"),
        P(None, "head"),
        P(None, "head"),
        P("head", None),
        P(),
        P(),
        P("batch", None),
    )
    out_specs = (P("batch", None), P("batch", None), P(None, "head"), P(None, "head"))
    return jax.shard_map(body, mesh=mesh, in_specs=in_specs, out_specs=out_specs, check_vma=False)
```

profile of v0, /device:TPU:0, one launch (start us, length us, event | category | flops | bytes accessed | tf_op | source)
XLA Modules:
  0.0 362.0 jit_solution(9636791249654251810)
XLA Ops:
  7.3 2.1 convolution_convert_fusion.1
  9.3 1.9 convolution_convert_fusion.2
  15.7 13.5 %while.26 = (s32[]{:T(128)}, bf16[2,512,192]{1,2,0:T(8,128)(2,1)}, f32[2,3,512,1]{2,1,3,0:T(4,128)}, bf16[2,512,192]{1,2,0:T(8,128)(2,1)S(1)}, s32[2]{0:T(128)},...) while((s32[]{:T(128)}, bf16[2,512,192]{1,2,0:T(8,128)(2,1)}, ...), condition=%wide.region_3.4_spmd, body=%wide.region_0.3_spmd.sunk | while | flops 210861056 | bytes 14995637 | solution.py:140
  15.7 1.2 dynamic_slice.52
  22.4 1.2 dynamic_slice.52
  30.2 3.3 fusion.49
  33.7 71.1 %all-reduce.6.cloned.1.call-done = f32[1024,768]{1,0:T(8,128)} async-done(((f32[1024,768]{1,0:T(8,128)}), f32[1024,768]{1,0:T(8,128)}) %all-reduce.6.cloned.1.call-update) | async-done | bytes 3145744 | tf_op jit(solution)/shard_map/psum | solution.py:144
  104.8 2.3 fusion.47
  107.8 7.4 %fusion.13 = (f32[1024,768]{1,0:T(8,128)S(1)}, f32[1024,768]{1,0:T(8,128)S(1)}) fusion(bf16[768,768]{1,0:T(8,128)(2,1)S(1)} %copy-done, f32[1024,768]{1,0:T(8,128)S(1)} %get-tuple-element.179, f32[768]{0:T(1024)S(1)} %copy-done.36, f32[1024]{0:T(1024)S(1)} %add_rsqrt_fusion.1, f32[1024]{0:T(1024)S(1)} %broadcast_multiply_fusion.5), kind=kOutput, calls=%fused_computation.35 | convolution fusion | flops 1259864064 | bytes 10628096 | tf_op jit(solution)/shard_map/dot_general | solution.py:147
  115.2 1.7 copy-done.8
  117.8 3.1 fusion.21
  122.3 67.3 %all-reduce.8.cloned.1.call-done = f32[1024,768]{1,0:T(8,128)} async-done(((f32[1024,768]{1,0:T(8,128)}), f32[1024,768]{1,0:T(8,128)}) %all-reduce.8.cloned.1.call-update) | async-done | bytes 3145744 | tf_op jit(solution)/shard_map/psum | solution.py:150
  189.7 3.6 fusion.46
  193.9 2.0 copy-done.7
  195.8 1.4 fusion.14
  198.4 7.8 %fusion.33 = f32[1024,768]{1,0:T(8,128)} fusion(bf16[768,768]{1,0:T(8,128)(2,1)S(1)} %copy-done, f32[1024,768]{1,0:T(8,128)} %copy-done.8, f32[1024,768]{1,0:T(8,128)} %copy-done.9, bf16[768,768]{1,0:T(8,128)(2,1)} %param.30, bf16[1024,768]{1,0:T(8,128)(2,1)S(1)} %copy-done.7, f32[1024,768]{1,0:T(8,128)} %copy-done.3, f32[1024]{0:T(1024)} %broadcast_multiply_fusion.2, ...), kind=kOutput, calls=%fused_computation.82 | convolution fusion | flops 2434793472 | bytes 16538624 | tf_op jit(solution)/shard_map/dot_general | solution.py:159
  206.6 68.4 %all-reduce.10.cloned.1.call-done = f32[1024,768]{1,0:T(8,128)} async-done(((f32[1024,768]{1,0:T(8,128)}), f32[1024,768]{1,0:T(8,128)}) %all-reduce.10.cloned.1.call-update) | async-done | bytes 3145744 | tf_op jit(solution)/shard_map/psum | solution.py:160
  275.1 5.8 %fusion.45 = (f32[1024]{0:T(1024)S(1)}, f32[1024]{0:T(1024)S(1)}, f32[1024,768]{1,0:T(8,128)S(1)}, bf16[1024,768]{1,0:T(8,128)(2,1)}) fusion(f32[1024]{0:T(1024)S(1)} %copy-done.24, f32[1024,768]{1,0:T(8,128)} %copy-done.2, f32[1024]{0:T(1024)S(1)} %copy-done.22, f32[768]{0:T(1024)S(1)} %copy-done.37, f32[1024,768]{1,0:T(8,128)} %all-reduce.10.cloned.1.call-done, ...), kind=kLoop, calls=%fused_computation.111 | loop fusion | flops 14940160 | bytes 15771648 | tf_op jit(solution)/shard_map/reduce_sum | solution.py:20
  280.9 2.4 subtract_multiply_fusion
  283.3 1.6 copy-done.5
  285.9 13.9 %while.27 = (s32[]{:T(128)}, bf16[2,512,192]{1,2,0:T(8,128)(2,1)S(1)}, bf16[2,512,192]{1,2,0:T(8,128)(2,1)S(1)}, bf16[2,512,192]{1,2,0:T(8,128)(2,1)S(1)}, bf16[...) while((s32[]{:T(128)}, ...), condition=%wide.region_17.18_spmd, body=%wide.region_15.17_spmd.sunk | while | flops 510884864 | bytes 28343456 | solution.py:164
  285.9 1.2 dynamic_slice.58
  289.3 1.1 multiply_reduce_fusion.6
  292.9 1.2 dynamic_slice.58
  296.2 1.1 multiply_reduce_fusion.6
  301.0 1.6 fusion.50
  303.1 1.4 fusion.53
  304.5 1.4 fusion.52
  306.5 2.0 add_convert_fusion.1
  308.9 37.8 %all-reduce = (f32[8,192]{1,0:T(8,128)}, f32[8,192]{1,0:T(8,128)}) all-reduce(f32[8,192]{1,0:T(8,128)S(1)} %convolution_multiply_fusion.7, f32[8,192]{1,0:T(8,128)S(1)} %convolution_multiply_fusion.6), channel_id=1, replica_groups=mesh['batch'=8,'head'=4] {'batch'}, use_global_device_ids=true, to_apply=%region_19.20 | all-reduce | flops 3072 | bytes 24576 | tf_op jit(solution)/shard_map/psum | solution.py:197
  346.8 4.8 %all-reduce.12.cloned.1.call-done = bf16[1024,768]{1,0:T(8,128)(2,1)} async-done(((bf16[1024,768]{1,0:T(8,128)(2,1)}), bf16[1024,768]{1,0:T(8,128)(2,1)}) %all-reduce.12.cloned.1.call-update) | async-done | bytes 1572880 | tf_op jit(solution)/shard_map/psum | solution.py:193
  351.6 3.8 %add_convert_fusion = bf16[1024,768]{1,0:T(8,128)(2,1)} fusion(f32[1024,768]{1,0:T(8,128)} %copy-done.5, bf16[1024,768]{1,0:T(8,128)(2,1)} %all-reduce.12.cloned.1.call-done), kind=kLoop, calls=%fused_computation.36 | loop fusion | flops 2359296 | bytes 6291456 | tf_op jit(solution)/shard_map/convert_element_type | solution.py:194
  (170 shorter events, 34.2 us)
Async XLA Ops:
  7.2 100.4 %copy-start = (bf16[768,768]{1,0:T(8,128)(2,1)S(1)}, bf16[768,768]{1,0:T(8,128)(2,1)}, u32[]{:S(2)}) copy-start(bf16[768,768]{1,0:T(8,128)(2,1)} %param.29) | copy-start | bytes 3538948
  7.2 4.1 %copy-start.4 = (bf16[1024,768]{1,0:T(8,128)(2,1)S(1)}, bf16[1024,768]{1,0:T(8,128)(2,1)}, u32[]{:S(2)}) copy-start(bf16[1024,768]{1,0:T(8,128)(2,1)} %param.19) | copy-start | bytes 4718596
  7.2 4.1 %copy-start.17 = (bf16[768,192]{0,1:T(8,128)(2,1)S(1)}, bf16[768,192]{0,1:T(8,128)(2,1)}, u32[]{:S(2)}) copy-start(bf16[768,192]{0,1:T(8,128)(2,1)} %param.22) | copy-start | bytes 884740
  7.2 97.6 %all-reduce.6.cloned.1.call-start = ((), (), s32[]{:S(2)}) async-start(), calls=%async_computation | async-start | bytes 6291456 | tf_op jit(solution)/shard_map/psum | solution.py:144
  7.3 4.7 %copy-start.34 = (bf16[8,192]{1,0:T(8,128)(2,1)S(1)}, bf16[8,192]{1,0:T(8,128)(2,1)}, u32[]{:S(2)}) copy-start(bf16[8,192]{1,0:T(8,128)(2,1)} %param.28) | copy-start | bytes 9220
  7.3 5.1 %copy-start.15 = (bf16[768,192]{0,1:T(8,128)(2,1)S(1)}, bf16[768,192]{0,1:T(8,128)(2,1)}, u32[]{:S(2)}) copy-start(bf16[768,192]{0,1:T(8,128)(2,1)} %param.23) | copy-start | bytes 884740
  33.5 156.2 %all-reduce.8.cloned.1.call-start = ((), (), s32[]{:S(2)}) async-start(), calls=%async_computation.1 | async-start | bytes 6291456 | tf_op jit(solution)/shard_map/psum | solution.py:150
  107.0 8.1 %copy-start.2 = (f32[1024,768]{1,0:T(8,128)}, f32[1024,768]{1,0:T(8,128)S(1)}, u32[]{:S(2)}) copy-start(f32[1024,768]{1,0:T(8,128)S(1)} %get-tuple-element.179) | copy-start | bytes 9437188
  107.1 82.6 %copy-start.21 = (f32[1024]{0:T(1024)}, f32[1024]{0:T(1024)S(1)}, u32[]{:S(2)}) copy-start(f32[1024]{0:T(1024)S(1)} %broadcast_multiply_fusion.5) | copy-start | bytes 12292
  107.7 81.9 %copy-start.23 = (f32[1024]{0:T(1024)}, f32[1024]{0:T(1024)S(1)}, u32[]{:S(2)}) copy-start(f32[1024]{0:T(1024)S(1)} %add_rsqrt_fusion.1) | copy-start | bytes 12292
  107.7 10.0 %copy-start.12 = (bf16[768,768]{1,0:T(8,128)(2,1)S(1)}, bf16[768,768]{1,0:T(8,128)(2,1)}, u32[]{:S(2)}) copy-start(bf16[768,768]{1,0:T(8,128)(2,1)} %param.30) | copy-start | bytes 3538948
  115.2 2.6 copy-start.9
  121.0 154.1 %all-reduce.10.cloned.1.call-start = ((), (), s32[]{:S(2)}) async-start(), calls=%async_computation.2 | async-start | bytes 6291456 | tf_op jit(solution)/shard_map/psum | solution.py:160
  193.3 3.9 %copy-start.3 = (f32[1024,768]{1,0:T(8,128)}, f32[1024,768]{1,0:T(8,128)S(1)}, u32[]{:S(2)}) copy-start(f32[1024,768]{1,0:T(8,128)S(1)} %get-tuple-element.177) | copy-start | bytes 9437188
  193.3 2.6 copy-start.7
  193.3 2.5 copy-start.29
  193.3 3.9 %copy-start.25 = (f32[1024]{0:T(1024)}, f32[1024]{0:T(1024)S(1)}, u32[]{:S(2)}) copy-start(f32[1024]{0:T(1024)S(1)} %broadcast_multiply_fusion.4) | copy-start | bytes 12292
  193.9 3.4 copy-start.31
  206.2 68.8 %copy-start.22 = (f32[1024]{0:T(1024)S(1)}, f32[1024]{0:T(1024)}, u32[]{:S(2)}) copy-start(f32[1024]{0:T(1024)} %copy-done.21) | copy-start | bytes 12292
  206.2 68.8 %copy-start.24 = (f32[1024]{0:T(1024)S(1)}, f32[1024]{0:T(1024)}, u32[]{:S(2)}) copy-start(f32[1024]{0:T(1024)} %copy-done.23) | copy-start | bytes 12292
  206.2 68.8 %copy-start.26 = (f32[1024]{0:T(1024)S(1)}, f32[1024]{0:T(1024)}, u32[]{:S(2)}) copy-start(f32[1024]{0:T(1024)} %copy-done.25) | copy-start | bytes 12292
  206.2 68.8 %copy-start.30 = (f32[1,4,2,128]{3,1,2,0:T(4,128)S(1)}, f32[1,4,2,128]{3,1,2,0:T(4,128)}, u32[]{:S(2)}) copy-start(f32[1,4,2,128]{3,1,2,0:T(4,128)} %copy.57) | copy-start | bytes 12292
  206.2 68.8 %copy-start.32 = (f32[1024]{0:T(1024)S(1)}, f32[1024]{0:T(1024)}, u32[]{:S(2)}) copy-start(f32[1024]{0:T(1024)} %copy-done.31) | copy-start | bytes 12292
  206.2 68.8 %copy-start.37 = (f32[768]{0:T(1024)S(1)}, f32[768]{0:T(1024)}, u32[]{:S(2)}) copy-start(f32[768]{0:T(1024)} %param.31) | copy-start | bytes 9220
  206.3 68.8 %copy-start.39 = (f32[768]{0:T(1024)S(1)}, f32[768]{0:T(1024)}, u32[]{:S(2)}) copy-start(f32[768]{0:T(1024)} %param.32) | copy-start | bytes 9220
  206.3 68.8 %copy-start.40 = (f32[1024]{0:T(1024)S(1)}, f32[1024]{0:T(1024)}, u32[]{:S(2)}) copy-start(f32[1024]{0:T(1024)} %broadcast_multiply_fusion.3) | copy-start | bytes 12292
  206.3 68.8 %copy-start.41 = (f32[1024]{0:T(1024)S(1)}, f32[1024]{0:T(1024)}, u32[]{:S(2)}) copy-start(f32[1024]{0:T(1024)} %broadcast_multiply_fusion.2) | copy-start | bytes 12292
  206.3 145.3 %all-reduce.12.cloned.1.call-start = ((), (), s32[]{:S(2)}) async-start(), calls=%async_computation.3 | async-start | bytes 3145728 | tf_op jit(solution)/shard_map/psum | solution.py:193
  280.9 4.1 %copy-start.14 = (bf16[192,768]{1,0:T(8,128)(2,1)S(1)}, bf16[192,768]{1,0:T(8,128)(2,1)}, u32[]{:S(2)}) copy-start(bf16[192,768]{1,0:T(8,128)(2,1)} %param.24) | copy-start | bytes 884740
  299.9 2.8 copy-start.35
  303.1 2.8 copy-start.18
  308.9 46.5 %copy-start.1 = (bf16[768,768]{1,0:T(8,128)(2,1)S(1)}, bf16[768,768]{1,0:T(8,128)(2,1)}, u32[]{:S(2)}) copy-start(bf16[768,768]{1,0:T(8,128)(2,1)} %param.29) | copy-start | bytes 3538948
  (16 other events, 24.0 us)
Sparse Core Ops, SparseCore 0:
  33.6 71.1 all-reduce.5
  121.1 68.5 all-reduce.7
  206.4 68.5 all-reduce.9
  308.6 42.9 all-reduce.11
where the time goes:
time: 363 us; the launch traced here: 362 us
  waiting for transfers between devices  212 us (58%)
  matrix products  47.7 us (13%)
  blocking collectives  37.8 us (10%)
  other arithmetic  29.1 us (8%)
  local copies, waits for them, and re-layouts  20.4 us (6%)
  between operations  14.5 us (4%)
    psum x1, waiting for transfers between devices, body(): attn = lax.psum(attn_part, 'head')  71.1 us
    psum x1, waiting for transfers between devices, body(): grad_h1 = grad_z2 + lax.psum(hidden_part, 'head')  68.4 us
    psum x1, waiting for transfers between devices, body(): ffn_total = lax.psum(ffn_part, 'head')  67.3 us
    psum x1, blocking collectives, body(): grad_b_query, grad_b_value = lax.psum((query_term, value_term), 'batch')  37.8 us
    dot_general x1, matrix products, body(): hidden_part = jnp.dot(grad_up, w_up.T, preferred_element_type=single_float)  7.76 us
    dot_general x1, matrix products, body(): up_pre = jnp.dot(hidden_low, w_up, preferred_element_type=single_float)  7.39 us
    unnamed x81, local copies, waits for them, and re-layouts  7.32 us
  transfers between devices with their start and end apart: 4, of which 4 were waited for; matrix products, arithmetic and copies ran while one was open for 0% of the time, Pallas kernels for 0%

commit v1 on v0

v1 whole, which is shorter than its diff:
```python
import functools

import jax
import jax.numpy as jnp
from jax import lax
from jax.experimental import pallas as pl
from jax.experimental.pallas import tpu as pltpu
from jax.sharding import PartitionSpec as P

HD = 64
BF16 = jnp.bfloat16
F32 = jnp.float32
MESH = pl.DeviceIdType.MESH

OUT, UP, DOWN, QKV = 0, 1, 5, 9
STAGES = ((0, 1), (1, 2), (3, 2), (5, 2), (7, 2), (9, 3))
OWN, SIB, FAR, FARSIB = 0, 1, 2, 3
INPUT_CHUNKS = 4


def dot(left, right, left_dim=1, right_dim=0):
    return lax.dot_general(
        left, right, (((left_dim,), (right_dim,)), ((), ())), preferred_element_type=F32
    )


def norm(z):
    centre = z - jnp.mean(z, axis=-1, keepdims=True)
    inverse = lax.rsqrt(jnp.mean(centre * centre, axis=-1, keepdims=True) + 1e-05)
    return centre * inverse, inverse


def norm_back(scaled, normed, inverse):
    return inverse * (
        scaled
        - jnp.mean(scaled, axis=-1, keepdims=True)
        - normed * jnp.mean(scaled * normed, axis=-1, keepdims=True)
    )


def flip(index, bit):
    return index + bit - 2 * bit * ((index // bit) % 2)


def kernel(
    batch_steps,
    lengths,
    tokens,
    w_query,
    w_key,
    w_value,
    w_out,
    w_up,
    w_down,
    down_query,
    down_value,
    up_query,
    up_value,
    gain_one,
    gain_two,
    cotangent,
    activations,
    input_grad,
    grad_adapters,
    x,
    raw,
    w,
    raw_down,
    raw_up,
    gains,
    cot,
    adapter_down,
    adapter_up,
    low,
    q,
    k,
    v,
    probs,
    ctx_out,
    ctx_in,
    normed_one,
    inverse_one,
    hidden,
    hidden_low,
    act,
    slope,
    total,
    grad_z2,
    grad_low,
    grad_z1,
    dctx_out,
    dctx_in,
    dq,
    dk,
    dv,
    part_out,
    part_in,
    rows_out,
    grads,
    grads_in,
    local_sem,
    send_sem,
    recv_sem,
):
    b = lax.axis_index("batch")
    h = lax.axis_index("head")
    core = h % 2
    seq = h // 2
    far_seq = 1 - seq
    part = b % 4
    sibling = (b, flip(h, 1))
    across = (b, flip(h, 2))
    diagonal = (b, 3 - h)
    x_peer = (flip(b, 1), h)
    z_peer = (flip(b, 2), h)
    batch_peers = [(flip(b, 1 << s), h) for s in range(batch_steps)]

    numbers = {}
    started = []
    local_numbers = {}

    def number(key):
        return numbers.setdefault(key, len(numbers))

    def copy(key, source, target, device):
        n = number(key)
        return pltpu.make_async_remote_copy(
            src_ref=source,
            dst_ref=target,
            send_sem=send_sem.at[n],
            recv_sem=recv_sem.at[n],
            device_id=device,
            device_id_type=MESH,
        )

    def send(key, source, target, device):
        c = copy(key, source, target, device)
        c.start()
        started.append(c)

    def arrived(key, target, device=None):
        copy(key, target, target, sibling).wait_recv()

    def load(key, source, target):
        c = pltpu.make_async_copy(
            source, target, local_sem.at[local_numbers.setdefault(key, len(local_numbers))]
        )
        c.start()
        return c

    raw_loads = [load(f"w{j}", r, raw.at[j]) for j, r in enumerate((w_query, w_key, w_value))]
    x_far_load = load("xf", tokens.at[pl.ds(2 * far_seq, 2)], x.at[pl.ds(2 * far_seq, 2)])
    small_loads = [
        load("s0", down_query, raw_down.at[0]),
        load("s1", down_value, raw_down.at[1]),
        load("s2", up_query, raw_up.at[0]),
        load("s3", up_value, raw_up.at[1]),
    ]
    x_own_load = load("xo", tokens.at[pl.ds(2 * seq, 2)], x.at[pl.ds(2 * seq, 2)])
    out_load = load("wo", w_out, w.at[OWN, pl.ds(OUT, 1)])
    up_load = load("wu", w_up, w.at[OWN, pl.ds(UP, 4)])
    down_load = load("wd", w_down, w.at[OWN, pl.ds(DOWN, 4)])
    late_loads = [
        load("g1", gain_one, gains.at[0]),
        load("g2", gain_two, gains.at[1]),
        load("co", cotangent.at[h], cot),
    ]

    barrier = pltpu.get_barrier_semaphore()
    peers = [sibling, across, diagonal] + batch_peers
    for peer in peers:
        pl.semaphore_signal(barrier, inc=1, device_id=peer, device_id_type=MESH)
    pl.semaphore_wait(barrier, len(peers))

    def rows_of(ref, first, count, index, third=None):
        if third is None:
            return ref.at[pl.ds(first, count), pl.ds(pl.multiple_of(48 * index, 16), 48)]
        return ref.at[pl.ds(first, count), pl.ds(pl.multiple_of(48 * index + 16 * third, 16), 16)]

    far = w.at[FAR]
    px, pz, pd = flip(part, 1), flip(part, 2), 3 - part

    def relay_start(s):
        if s >= len(STAGES):
            return
        first, count = STAGES[s]
        if first >= QKV:
            source, at = w.at[OWN], first
        elif first >= DOWN:
            source, at = w_down, first - DOWN
        elif first >= UP:
            source, at = w_up, first - UP
        else:
            source, at = w_out, first
        send(("y", s), rows_of(source, at, count, part), rows_of(far, first, count, part), across)
        send(
            ("y3", s),
            rows_of(source, at, count, pd, 0),
            rows_of(far, first, count, pd, 0),
            across,
        )

    def relay_one(s):
        first, count = STAGES[s]
        mine = rows_of(far, first, count, part)
        arrived(("y", s), mine)
        send(("x", s), mine, mine, x_peer)
        send(("z", s), mine, mine, z_peer)
        relay_start(s + 2)

    def relay_two(s):
        first, count = STAGES[s]
        arrived(("x", s), rows_of(far, first, count, px))
        piece = rows_of(far, first, count, px, 2)
        send(("z3", s), piece, piece, z_peer)
        arrived(("z", s), rows_of(far, first, count, pz))
        piece = rows_of(far, first, count, pz, 1)
        send(("x3", s), piece, piece, x_peer)

    def relay_three(s):
        first, count = STAGES[s]
        arrived(("y3", s), rows_of(far, first, count, pd, 0))
        arrived(("x3", s), rows_of(far, first, count, pd, 1))
        arrived(("z3", s), rows_of(far, first, count, pd, 2))
        if first < QKV:
            items = pl.ds(first, count)
            send(("c", s), w.at[FAR, items], w.at[FARSIB, items], sibling)

    def relay_end(s):
        first, count = STAGES[s]
        arrived(("c", s), w.at[FARSIB, pl.ds(first, count)])

    relay_start(0)
    relay_start(1)
    send("so", w_out, w.at[SIB, pl.ds(OUT, 1)], sibling)
    send("su", w_up, w.at[SIB, pl.ds(UP, 4)], sibling)
    send("sd", w_down, w.at[SIB, pl.ds(DOWN, 4)], sibling)

    for c in small_loads:
        c.wait()
    adapter_down[...] = jnp.concatenate([raw_down[0], raw_down[1]] * 2, axis=1)
    nothing = jnp.zeros((8, 192), F32)
    adapter_up[0, 0] = jnp.concatenate([raw_up[0].astype(F32), nothing], axis=0)
    adapter_up[0, 1] = jnp.concatenate([nothing, raw_up[1].astype(F32)], axis=0)
    send("b", adapter_up.at[0], adapter_up.at[1], across)

    for j in range(3):
        raw_loads[j].wait()
        w[OWN, QKV + j] = raw[j].T

    def project(rows, which, slot, store):
        xs = x[pl.ds(2 * rows, 2)].reshape(512, 768)
        lows = dot(xs, adapter_down[:, :16]).astype(BF16)
        ups = adapter_up[0 if slot == OWN else 1].astype(BF16)
        if store:
            low[...] = lows
        for ref, j in ((q, 0), (k, 1), (v, 2)):
            full = dot(xs, w[slot, QKV + j], 1, 1)
            if j != 1:
                full = full + 2.0 * dot(lows, ups[j // 2])
            full = full.astype(BF16)
            for head in range(3):
                ref[which, head] = full[:, head * HD : (head + 1) * HD]

    def attend(rows, which, context):
        keep = lax.broadcasted_iota(jnp.int32, (512, 1), 0) < lengths[rows]
        for head in range(3):
            scores = jnp.where(keep, dot(k[which, head], q[which, head], 1, 1) * 0.125, -1e30)
            exponent = jnp.exp(scores - jnp.max(scores, axis=0, keepdims=True))
            weights = exponent * (1.0 / jnp.sum(exponent, axis=0, keepdims=True))
            weights = weights.astype(BF16)
            probs[which, head] = weights
            if context is not None:
                out = dot(v[which, head], weights, 0, 0).astype(BF16)
                columns = slice(head * HD, (head + 1) * HD)
                ctx_out[context, 0, columns] = out[:, :256]
                ctx_out[context, 1, columns] = out[:, 256:]

    x_far_load.wait()
    project(far_seq, 1, OWN, False)
    relay_one(0)
    attend(far_seq, 1, 1)
    send("cy", ctx_out.at[1, core], ctx_in.at[FAR], across)
    send("cd", ctx_out.at[1, 1 - core], ctx_in.at[FARSIB], diagonal)
    relay_one(1)
    relay_two(0)
    x_own_load.wait()
    project(seq, 0, OWN, True)
    relay_three(0)
    attend(seq, 0, 0)
    send("cc", ctx_out.at[0, 1 - core], ctx_in.at[SIB], sibling)
    ctx_in[OWN] = ctx_out[0, core]
    relay_one(2)
    relay_two(1)

    out_load.wait()
    for c in late_loads:
        c.wait()
    arrived("so", w.at[SIB, pl.ds(OUT, 1)])
    relay_end(0)
    arrived("cc", ctx_in.at[SIB])
    arrived("cy", ctx_in.at[FAR])
    arrived("cd", ctx_in.at[FARSIB])
    all_out = w[:, OUT].reshape(768, 768)
    attn = dot(ctx_in[...].reshape(768, 256), all_out, 0, 0)
    n1, r1 = norm(x[h].astype(F32) + attn)
    normed_one[...] = n1
    inverse_one[...] = r1
    h1 = n1 * gains[0]
    hidden[...] = h1
    hidden_low[...] = h1.astype(BF16)

    def go_up(slot):
        up = dot(hidden_low[...], w[slot, UP : UP + 4].reshape(768, 768))
        phi = 0.5 * (1.0 + lax.erf(up * 0.7071067811865476))
        slope[slot] = phi + up * (0.3989422804014327 * jnp.exp(-0.5 * up * up))
        act[slot] = (up * phi).astype(BF16)

    def go_down(slot):
        return dot(act[slot], w[slot, DOWN : DOWN + 4].reshape(768, 768))

    up_load.wait()
    down_load.wait()
    go_up(OWN)
    total[...] = hidden[...] + go_down(OWN)
    relay_three(1)
    arrived("su", w.at[SIB, pl.ds(UP, 4)])
    arrived("sd", w.at[SIB, pl.ds(DOWN, 4)])
    go_up(SIB)
    total[...] += go_down(SIB)
    relay_one(3)
    relay_two(2)
    relay_three(2)
    go_up(FAR)
    relay_one(4)
    relay_two(3)
    relay_end(1)
    relay_end(2)
    go_up(FARSIB)
    relay_three(3)
    relay_one(5)
    relay_two(4)
    relay_three(4)
    total[...] += go_down(FAR)
    relay_end(3)
    relay_end(4)
    z2 = total[...] + go_down(FARSIB)

    n2, r2 = norm(z2)
    position = lax.broadcasted_iota(jnp.int32, (256, 1), 0) + 256 * core
    valid = (position < lengths[seq]).astype(F32)
    rows_out[0] = (valid * (n2 * gains[1])).astype(BF16)
    send("ay", rows_out.at[0], activations.at[h], across)
    send("ac", rows_out.at[0], activations.at[h], sibling)
    act_store = load("a", rows_out.at[0], activations.at[h])
    d_z2 = norm_back(cot[...].astype(F32) * valid * gains[1], n2, r2)
    grad_low[...] = d_z2.astype(BF16)
    grad_z2[...] = d_z2

    def back(slot):
        d_act = dot(grad_low[...], w[slot, DOWN : DOWN + 4].reshape(768, 768), 1, 1)
        d_up = (d_act * slope[slot]).astype(BF16)
        grad_z2[...] += dot(d_up, w[slot, UP : UP + 4].reshape(768, 768), 1, 1)

    back(OWN)
    back(SIB)
    relay_two(5)
    back(FAR)
    back(FARSIB)

    d_z1 = norm_back(grad_z2[...] * gains[0], normed_one[...], inverse_one[...])
    grad_z1[...] = d_z1
    all_out = w[:, OUT].reshape(768, 768)
    d_ctx = dot(all_out, d_z1.astype(BF16), 1, 1).astype(BF16)
    dctx_out[...] = d_ctx.reshape(4, 192, 256)
    send("d0", dctx_out.at[SIB], dctx_in.at[0, core], sibling)
    send("d1", dctx_out.at[FARSIB], dctx_in.at[1, core], sibling)
    dctx_in[0, core] = dctx_out[OWN]
    dctx_in[1, core] = dctx_out[FAR]

    relay_three(5)
    arrived("b", adapter_up.at[1])
    project(seq, 1, FAR, False)
    attend(seq, 1, None)
    arrived("ay", activations.at[flip(h, 2)])
    send("ar", activations.at[flip(h, 2)], activations.at[flip(h, 2)], sibling)
    arrived("d0", dctx_in.at[0, 1 - core])
    arrived("d1", dctx_in.at[1, 1 - core])

    def attend_back(which):
        for head in range(3):
            columns = slice(head * HD, (head + 1) * HD)
            d_out = jnp.concatenate(
                [dctx_in[which, 0, columns], dctx_in[which, 1, columns]], axis=1
            )
            weights = probs[which, head]
            probability = weights.astype(F32)
            d_weights = dot(v[which, head], d_out)
            mean = jnp.sum(probability * d_weights, axis=0, keepdims=True)
            d_scores = (probability * (d_weights - mean)).astype(BF16)
            d_value = dot(weights, d_out, 1, 1).astype(BF16)
            d_key = (0.125 * dot(d_scores, q[which, head])).astype(BF16)
            d_query = (0.125 * dot(k[which, head], d_scores, 0, 0)).astype(BF16)
            for half in range(2):
                span = slice(256 * half, 256 * half + 256)
                dv[which, half, :, columns] = d_value[span]
                dk[which, half, :, columns] = d_key[span]
                dq[which, half, columns] = d_query[:, span]

    attend_back(0)
    attend_back(1)

    lows = low[...].reshape(2, 256, 16)

    def adapter_grads(which):
        return [
            2.0
            * (
                dot(lows[0], dq[which, 0], 0, 1) + dot(lows[1], dq[which, 1], 0, 1)
                if j == 0
                else dot(lows[0], dv[which, 0], 0, 0) + dot(lows[1], dv[which, 1], 0, 0)
            )
            for j in range(2)
        ]

    def input_part(half):
        part_sum = 0.0
        d_low = 0.0
        for which, slot in ((0, OWN), (1, FAR)):
            part_sum = part_sum + dot(dq[which, half], w[slot, QKV], 0, 0)
            part_sum = part_sum + dot(dk[which, half], w[slot, QKV + 1])
            part_sum = part_sum + dot(dv[which, half], w[slot, QKV + 2])
            ups = adapter_up[which].astype(BF16)
            d_low = d_low + dot(dq[which, half], ups[0], 0, 1) + dot(dv[which, half], ups[1], 1, 1)
        d_low = 2.0 * d_low
        coarse = d_low.astype(BF16)
        fine = (d_low - coarse.astype(F32)).astype(BF16)
        both = jnp.concatenate([coarse, fine], axis=1)
        return part_sum + dot(both, adapter_down[...], 1, 1)

    part_out[...] = input_part(1 - core).astype(BF16)
    send("p", part_out, part_in, sibling)
    grad_z1[...] += input_part(core)
    arrived("p", part_in)
    span = 256 // INPUT_CHUNKS
    for t in range(INPUT_CHUNKS):
        rows = pl.ds(span * t, span)
        rows_out[1, rows] = (grad_z1[rows] + part_in[rows].astype(F32)).astype(BF16)
        send(("iy", t), rows_out.at[1, rows], input_grad.at[h, rows], across)
    send("ic", rows_out.at[1], input_grad.at[h], sibling)
    grad_store = load("i", rows_out.at[1], input_grad.at[h])

    for which in range(2):
        for j, term in enumerate(adapter_grads(which)):
            grads[which, j] = term
    send("g", grads.at[1], grads_in.at[0], across)
    arrived("g", grads_in.at[0])
    grads[0] += grads_in[0]
    for s in range(batch_steps):
        source = 0 if s == 0 else 1 + s
        send(("g", s), grads.at[source], grads_in.at[1 + s], batch_peers[s])
        arrived(("g", s), grads_in.at[1 + s])
        grads[2 + s] = grads[source] + grads_in[1 + s]
    final = grads[1 + batch_steps]
    grad_adapters[0] = final[0, 0:8]
    grad_adapters[1] = final[1, 8:16]

    for t in range(INPUT_CHUNKS):
        rows = pl.ds(span * t, span)
        block = input_grad.at[flip(h, 2), rows]
        arrived(("iy", t), block)
        send(("ir", t), block, block, sibling)
    arrived("ac", activations.at[flip(h, 1)])
    arrived("ar", activations.at[3 - h])
    arrived("ic", input_grad.at[flip(h, 1)])
    for t in range(INPUT_CHUNKS):
        arrived(("ir", t), input_grad.at[3 - h, pl.ds(span * t, span)])
    act_store.wait()
    grad_store.wait()
    for c in started:
        c.wait_send()


def body(batch_steps, *given):
    (
        tokens,
        lengths,
        w_query,
        w_key,
        w_value,
        w_out,
        down_query,
        down_value,
        up_query,
        up_value,
        w_up,
        w_down,
        gain_attn,
        gain_ffn,
        cotangent,
    ) = given
    anywhere = pl.BlockSpec(memory_space=pl.ANY)
    vmem = pltpu.VMEM
    activations, input_grad, grad_adapters = pl.pallas_call(
        functools.partial(kernel, batch_steps),
        out_shape=(
            jax.ShapeDtypeStruct((4, 256, 768), BF16),
            jax.ShapeDtypeStruct((4, 256, 768), BF16),
            jax.ShapeDtypeStruct((2, 8, 192), F32),
        ),
        in_specs=[pl.BlockSpec(memory_space=pltpu.SMEM)] + [anywhere] * 14,
        out_specs=(anywhere, anywhere, pl.BlockSpec(memory_space=pltpu.VMEM)),
        scratch_shapes=[
            vmem((4, 256, 768), BF16),
            vmem((3, 768, 192), BF16),
            vmem((4, 12, 192, 768), BF16),
            vmem((2, 768, 8), BF16),
            vmem((2, 8, 192), BF16),
            vmem((2, 1, 768), F32),
            vmem((256, 768), BF16),
            vmem((768, 32), BF16),
            vmem((2, 2, 16, 192), F32),
            vmem((512, 16), BF16),
            vmem((2, 3, 512, 64), BF16),
            vmem((2, 3, 512, 64), BF16),
            vmem((2, 3, 512, 64), BF16),
            vmem((2, 3, 512, 512), BF16),
            vmem((2, 2, 192, 256), BF16),
            vmem((4, 192, 256), BF16),
            vmem((256, 768), F32),
            vmem((256, 1), F32),
            vmem((256, 768), F32),
            vmem((256, 768), BF16),
            vmem((4, 256, 768), BF16),
            vmem((4, 256, 768), F32),
            vmem((256, 768), F32),
            vmem((256, 768), F32),
            vmem((256, 768), BF16),
            vmem((256, 768), F32),
            vmem((4, 192, 256), BF16),
            vmem((2, 2, 192, 256), BF16),
            vmem((2, 2, 192, 256), BF16),
            vmem((2, 2, 256, 192), BF16),
            vmem((2, 2, 256, 192), BF16),
            vmem((256, 768), BF16),
            vmem((256, 768), BF16),
            vmem((2, 256, 768), BF16),
            vmem((2 + batch_steps, 2, 16, 192), F32),
            vmem((1 + batch_steps, 2, 16, 192), F32),
            pltpu.SemaphoreType.DMA((20,)),
            pltpu.SemaphoreType.DMA((80,)),
            pltpu.SemaphoreType.DMA((80,)),
        ],
        compiler_params=pltpu.CompilerParams(
            collective_id=0, has_side_effects=True, vmem_limit_bytes=60 * 1024 * 1024
        ),
        cost_estimate=pl.CostEstimate(
            flops=11_000_000_000, bytes_accessed=20_000_000, transcendentals=4_000_000
        ),
    )(
        lengths,
        tokens.reshape(4, 256, 768),
        w_query,
        w_key,
        w_value,
        w_out.reshape(1, 192, 768),
        w_up.reshape(4, 192, 768),
        w_down.reshape(4, 192, 768),
        down_query,
        down_value,
        up_query,
        up_value,
        gain_attn.reshape(1, 768),
        gain_ffn.reshape(1, 768),
        cotangent.reshape(4, 256, 768),
    )
    return (
        activations.reshape(tokens.shape),
        input_grad.reshape(tokens.shape),
        grad_adapters[0],
        grad_adapters[1],
    )


def solution(mesh):
    batch_steps = mesh.shape["batch"].bit_length() - 1
    in_specs = (
        P("batch", None),
        P("batch"),
        P(None, "head"),
        P(None, "head"),
        P(None, "head"),
        P("head", None),
        P(),
        P(),
        P(None, "head"),
        P(None, "head"),
        P(None, "head"),
        P("head", None),
        P(),
        P(),
        P("batch", None),
    )
    out_specs = (P("batch", None), P("batch", None), P(None, "head"), P(None, "head"))
    return jax.shard_map(
        functools.partial(body, batch_steps),
        mesh=mesh,
        in_specs=in_specs,
        out_specs=out_specs,
        check_vma=False,
    )
```

time: 363 us -> 104 us (0.29)
  waiting for transfers between devices: 212 us -> 0 us
  Pallas kernels: 0 us -> 87.5 us
  matrix products: 47.7 us -> 0 us
  blocking collectives: 37.8 us -> 0 us
  other arithmetic: 29.1 us -> 0 us
  between operations: 14.5 us -> 0.65 us
  local copies, waits for them, and re-layouts: 20.4 us -> 15.5 us
    psum x4 -> x0, waiting for transfers between devices: 212 us -> none  [the longest x1 71.1 us: body(): attn = lax.psum(attn_part, 'head')]
    pallas_call x0 -> x1, Pallas kernels: none -> 87.5 us  [body(): pl.pallas_call(functools.partial(kernel, batch_steps), out_shape=(jax.Sha...]
    dot_general x35 -> x0, matrix products: 47.7 us -> none  [the longest x1 7.76 us: body(): hidden_part = jnp.dot(grad_up, w_up.T, preferred_element_type=single_float)]
    psum x1 -> x0, blocking collectives: 37.8 us -> none  [body(): grad_b_query, grad_b_value = lax.psum((query_term, value_term), 'batch')]
    reduce_sum x8 -> x0, other arithmetic: 15.4 us -> none  [the longest x2 7.16 us: norm_back(): jnp.mean(scaled, axis=-1, keepdims=True)]
    dynamic_slice x16 -> x0, local copies, waits for them, and re-layouts: 7.08 us -> none  [body(): context, logsum = lax.map(attend, (query_seq, key_seq, value_seq, lengths))]
    convert_element_type x3 -> x0, other arithmetic: 5.49 us -> none  [the longest x1 3.83 us: body(): input_grad = (grad_z1 + lax.psum(input_part.astype(jnp.bfloat16), 'head')...]
    unnamed x81 -> x11, local copies, waits for them, and re-layouts: 7.32 us -> 11.6 us
  transfers between devices with their start and end apart: 4 -> 0, of which waited for: 4 -> 0; matrix products, arithmetic and copies ran while one was open for 0% -> 0% of each run, Pallas kernels for 0% -> 0%
where the time goes in v1:
time: 104 us
  Pallas kernels  87.5 us (84%)
  local copies, waits for them, and re-layouts  15.5 us (15%)
    pallas_call x1, Pallas kernels, body(): pl.pallas_call(functools.partial(kernel, batch_steps), out_shape=(jax.Sha...  87.5 us
    unnamed x11, local copies, waits for them, and re-layouts  11.6 us

profile of v1, /device:TPU:0, one launch (start us, length us, event | category | flops | bytes accessed | tf_op | source)
XLA Modules:
  0.0 103.7 jit_solution(14039466956468355434)
XLA Ops:
  0.6 0.0 copy-start.1
  0.6 1.3 %reshape.39.gain_one = f32[1,768]{1,0:T(1,128)} reshape(f32[768]{0:T(1024)} %param.27) | data formatting | bytes 6144 | tf_op jit(solution)/shard_map/reshape | solution.py:573
  2.0 1.3 %reshape.40.gain_two = f32[1,768]{1,0:T(1,128)} reshape(f32[768]{0:T(1024)} %param.28) | data formatting | bytes 6144 | tf_op jit(solution)/shard_map/reshape | solution.py:574
  3.2 1.5 %copy.22.down_query = bf16[768,8]{1,0:T(8,128)(2,1)} copy(bf16[768,8]{0,1:T(8,128)(2,1)} %param.21) | data formatting | bytes 24576 | tf_op args[6]
  4.7 1.5 %copy.23.down_value = bf16[768,8]{1,0:T(8,128)(2,1)} copy(bf16[768,8]{0,1:T(8,128)(2,1)} %param.22) | data formatting | bytes 24576 | tf_op args[7]
  6.2 1.9 %copy.19.w_query = bf16[768,192]{1,0:T(8,128)(2,1)} copy(bf16[768,192]{0,1:T(8,128)(2,1)} %param.17) | data formatting | bytes 589824 | tf_op args[2]
  8.1 1.9 %copy.20.w_key = bf16[768,192]{1,0:T(8,128)(2,1)} copy(bf16[768,192]{0,1:T(8,128)(2,1)} %param.18) | data formatting | bytes 589824 | tf_op args[3]
  10.0 0.0 copy-done.1
  10.0 0.9 copy.21.w_value
  10.9 87.5 %shard_map.174 = (bf16[4,256,768]{2,1,0:T(8,128)(2,1)}, bf16[4,256,768]{2,1,0:T(8,128)(2,1)}, f32[2,8,192]{2,1,0:T(8,128)}) custom-call(s32[2]{0:T(128)} %lengths.1, bf16[4,256,768]{2,1,0:T(8,128)(2,1)} %bitcast.13, bf16[768,192]{1,0:T(8,128)(2,1)} %copy.19.w_query, bf16[768,192]{1,0:T(8,128)(2,1)} %copy.20.w_key, bf16[768,192]{1,0:T(8,128)(2,1)} %copy.21.w_value, ...), custom_call_target="tpu_custom_call" | custom-call | flops 11000000512 | bytes 20000000 | tf_op jit(solution)/shard_map/pallas_call | solution.py:504
  98.5 1.3 %slice_bitcast_fusion = (f32[8,192]{1,0:T(8,128)}, f32[8,192]{1,0:T(8,128)}) fusion(f32[2,8,192]{2,1,0:T(8,128)} %get-tuple-element.9), kind=kLoop, calls=%fused_computation | loop fusion | bytes 24576 | tf_op jit(solution)/shard_map/squeeze | solution.py:581
  99.8 0.0 copy-start
  99.8 2.8 %copy.26 = bf16[1024,768]{1,0:T(8,128)(2,1)} copy(bf16[1024,768]{1,0:T(8,128)(2,1)} %bitcast.12) | data formatting | bytes 3145728
  102.6 0.0 copy-done
  102.6 1.1 %copy.27 = bf16[1024,768]{1,0:T(8,128)(2,1)} copy(bf16[1024,768]{1,0:T(8,128)(2,1)S(1)} %bitcast.11) | data formatting | bytes 3145728
Async XLA Ops:
  0.6 9.4 %copy-start.1 = (bf16[768,192]{0,1:T(8,128)(2,1)S(1)}, bf16[768,192]{0,1:T(8,128)(2,1)}, u32[]{:S(2)}) copy-start(bf16[768,192]{0,1:T(8,128)(2,1)} %param.19) | copy-start | bytes 884740
  99.8 2.8 %copy-start = (bf16[4,256,768]{2,1,0:T(8,128)(2,1)S(1)}, bf16[4,256,768]{2,1,0:T(8,128)(2,1)}, u32[]{:S(2)}) copy-start(bf16[4,256,768]{2,1,0:T(8,128)(2,1)} %get-tuple-element.8) | copy-start | bytes 4718596

commit v2 on v1

v2 whole, which is shorter than its diff:
```python
import functools

import jax
import jax.numpy as jnp
from jax import lax
from jax.experimental import pallas as pl
from jax.experimental.pallas import tpu as pltpu
from jax.sharding import PartitionSpec as P

HD = 64
BF16 = jnp.bfloat16
F32 = jnp.float32
MESH = pl.DeviceIdType.MESH

OUT, UP, DOWN, QKV, ADAPTER = 0, 1, 5, 9, 12
OWN, SIB, FAR, FARSIB = 0, 1, 2, 3
OVER_Y = (32, 16) * 6
GROUPS = ((0, 1), (1, 4), (5, 2), (7, 2), (9, 3))
CHUNKS = ((0, 128), (128, 64), (192, 64))
SEND_GROUPS = ("y", "x", "z", "t", "d", "c", "w", "ctx", "dctx", "rows", "b", "g")


def dot(left, right, left_dim=1, right_dim=0):
    return lax.dot_general(
        left, right, (((left_dim,), (right_dim,)), ((), ())), preferred_element_type=F32
    )


def norm(z):
    centre = z - jnp.mean(z, axis=-1, keepdims=True)
    inverse = lax.rsqrt(jnp.mean(centre * centre, axis=-1, keepdims=True) + 1e-05)
    return centre * inverse, inverse


def norm_back(scaled, normed, inverse):
    return inverse * (
        scaled
        - jnp.mean(scaled, axis=-1, keepdims=True)
        - normed * jnp.mean(scaled * normed, axis=-1, keepdims=True)
    )


def flip(index, bit):
    return index + bit - 2 * bit * ((index // bit) % 2)


def kernel(
    batch_steps,
    lengths,
    tokens,
    w_query,
    w_key,
    w_value,
    w_out,
    w_up,
    w_down,
    down_query,
    down_value,
    up_query,
    up_value,
    gain_one,
    gain_two,
    cotangent,
    activations,
    input_grad,
    grads_out,
    x,
    w,
    raw_down,
    raw_up,
    gains,
    cot,
    adapter_up,
    low,
    qkv,
    probs,
    ctx_out,
    ctx_in,
    normed_one,
    inverse_one,
    hidden,
    hidden_low,
    act,
    slope,
    total,
    grad_z1,
    dctx_out,
    dctx_in,
    grad_qkv,
    part_out,
    part_in,
    grads,
    grads_in,
    local_sem,
    send_sem,
    recv_sem,
):
    b = lax.axis_index("batch")
    h = lax.axis_index("head")
    core = h % 2
    seq = h // 2
    far_seq = 1 - seq
    part = b % 4
    sibling = (b, flip(h, 1))
    across = (b, flip(h, 2))
    diagonal = (b, 3 - h)
    x_peer = (flip(b, 1), h)
    z_peer = (flip(b, 2), h)
    xz_peer = (flip(flip(b, 1), 2), h)
    batch_peers = [(flip(b, 1 << s), h) for s in range(batch_steps)]

    barrier = pltpu.get_barrier_semaphore()
    peers = [sibling, across, diagonal, xz_peer] + batch_peers
    for peer in peers:
        pl.semaphore_signal(barrier, inc=1, device_id=peer, device_id_type=MESH)

    recv_numbers = {}
    local_numbers = {}

    def copy(group, key, source, target, device):
        number = recv_numbers.setdefault(key, len(recv_numbers))
        return pltpu.make_async_remote_copy(
            src_ref=source,
            dst_ref=target,
            send_sem=send_sem.at[SEND_GROUPS.index(group)],
            recv_sem=recv_sem.at[number],
            device_id=device,
            device_id_type=MESH,
        )

    def send(group, key, source, target, device):
        copy(group, key, source, target, device).start()

    def arrived(key, target):
        copy("y", key, target, target, sibling).wait_recv()

    def sent(group, ref):
        copy(group, ("y", 0), ref, ref, sibling).wait_send()

    def local(key, source, target):
        number = local_numbers.setdefault(key, len(local_numbers))
        return pltpu.make_async_copy(source, target, local_sem.at[number])

    def load(key, source, target):
        local(key, source, target).start()

    def loaded(key, target):
        local(key, target, target).wait()

    for j, ref in enumerate((w_query, w_key, w_value)):
        load("qkv", ref, w.at[OWN, QKV + j])
    load("far", tokens.at[pl.ds(2 * far_seq, 2)], x.at[pl.ds(2 * far_seq, 2)])
    load("downs", down_query, raw_down.at[0])
    load("downs", down_value, raw_down.at[1])
    load("ups", up_query, raw_up.at[0])
    load("ups", up_value, raw_up.at[1])
    load("own", tokens.at[pl.ds(2 * seq, 2)], x.at[pl.ds(2 * seq, 2)])
    load("w", w_out, w.at[OWN, pl.ds(OUT, 1)])
    load("w", w_up, w.at[OWN, pl.ds(UP, 4)])
    load("w", w_down, w.at[OWN, pl.ds(DOWN, 4)])
    load("one", gain_one, gains.at[0])
    load("two", gain_two, gains.at[1])
    load("cot", cotangent.at[h], cot)

    far = w.at[FAR]
    pd = 3 - part
    group_of = {}
    for first, count in GROUPS:
        for item in range(first, first + count):
            group_of[item] = first

    def rows_of(ref, item, index, start=0, count=48):
        return ref.at[item, pl.ds(pl.multiple_of(48 * index + start, 16), count)]

    def source_of(item):
        if item >= QKV:
            return w.at[OWN], item
        if item >= DOWN:
            return w_down, item - DOWN
        if item >= UP:
            return w_up, item - UP
        return w_out, item

    def send_part(*items):
        for item in items:
            source, at = source_of(item)
            mine, theirs = rows_of(source, at, part), rows_of(far, item, part)
            send("y", ("y", item), mine, theirs, across)

    def send_rest(*items):
        for item in items:
            source, at = source_of(item)
            count = OVER_Y[item]
            mine, theirs = rows_of(source, at, pd, 0, count), rows_of(far, item, pd, 0, count)
            send("t", ("f", group_of[item]), mine, theirs, across)

    def relay(*items):
        for item in items:
            mine = rows_of(far, item, part)
            arrived(("y", item), mine)
            key = ("f", group_of[item])
            send("x", key, mine, mine, x_peer)
            send("z", key, mine, mine, z_peer)
            count = OVER_Y[item]
            rest = rows_of(far, item, part, count, 48 - count)
            send("d", key, rest, rest, xz_peer)

    def collect(group):
        first, count = GROUPS[group]
        items = pl.ds(first, count)
        arrived(("f", first), w.at[FAR, items, pl.ds(0, 144)])
        if first < QKV:
            send("c", ("c", first), w.at[FAR, items], w.at[FARSIB, items], sibling)

    def collect_sibling(group):
        first, count = GROUPS[group]
        arrived(("c", first), w.at[FARSIB, pl.ds(first, count)])

    pl.semaphore_wait(barrier, len(peers))
    send_part(0, 1)
    send_rest(0)
    send_part(2, 3, 4, 5)
    send("w", "so", w_out, w.at[SIB, pl.ds(OUT, 1)], sibling)
    send("w", "su", w_up, w.at[SIB, pl.ds(UP, 4)], sibling)
    send("w", "sd", w_down, w.at[SIB, pl.ds(DOWN, 4)], sibling)

    loaded("downs", raw_down)
    loaded("ups", raw_up)
    downs = jnp.concatenate([raw_down[0].astype(F32), raw_down[1].astype(F32)] * 2, axis=0)
    w[OWN, ADAPTER, :32] = downs.astype(BF16)
    w[FAR, ADAPTER, :32] = downs.astype(BF16)
    nothing = jnp.zeros((8, 192), F32)
    adapter_up[0, :, :192] = jnp.concatenate([raw_up[0].astype(F32), nothing], axis=0)
    adapter_up[0, :, 192:384] = jnp.zeros((16, 192), F32)
    adapter_up[0, :, 384:] = jnp.concatenate([nothing, raw_up[1].astype(F32)], axis=0)
    send("b", "b", adapter_up.at[0], adapter_up.at[1], across)

    def adapted(slot, count):
        return w[slot, QKV:].reshape(768, 768)[:count]

    def project(rows, which, slot, store):
        full = dot(adapted(slot, 592), x[pl.ds(2 * rows, 2)].reshape(512, 768), 1, 1)
        lows = full[576:].astype(BF16)
        ups = adapter_up[0 if slot == OWN else 1].astype(BF16)
        if store:
            low[...] = lows
        query = full[:192] + 2.0 * dot(ups[:, :192], lows, 0, 0)
        value = full[384:576] + 2.0 * dot(ups[:, 384:], lows, 0, 0)
        qkv[which, :192] = query.astype(BF16)
        qkv[which, 192:384] = full[192:384].astype(BF16)
        qkv[which, 384:] = value.astype(BF16)

    def head_rows(j, head):
        return slice(192 * j + HD * head, 192 * j + HD * (head + 1))

    def attend(rows, which, context):
        position = lax.broadcasted_iota(jnp.int32, (512, 1), 0)
        bias = jnp.where(position < lengths[rows], 0.0, -1e30)
        for head in range(3):
            query = qkv[which, head_rows(0, head)] * jnp.asarray(0.125, BF16)
            scores = dot(qkv[which, head_rows(1, head)], query, 0, 0) + bias
            exponent = jnp.exp(scores - jnp.max(scores, axis=0, keepdims=True))
            weights = exponent * (1.0 / jnp.sum(exponent, axis=0, keepdims=True))
            probs[which, head] = weights.astype(BF16)
        if context is None:
            return
        for head in range(3):
            out = dot(qkv[which, head_rows(2, head)], probs[which, head]).astype(BF16)
            ctx_out[context, 0, head_rows(0, head)] = out[:, :256]
            ctx_out[context, 1, head_rows(0, head)] = out[:, 256:]

    loaded("qkv", w.at[OWN, pl.ds(QKV, 3)])
    loaded("far", x.at[pl.ds(2 * far_seq, 2)])
    project(far_seq, 1, OWN, False)
    attend(far_seq, 1, 1)
    send("ctx", "ctx", ctx_out.at[1, core], ctx_in.at[FAR], across)
    send("ctx", "ctx", ctx_out.at[1, 1 - core], ctx_in.at[FARSIB], diagonal)
    relay(0)
    loaded("own", x.at[pl.ds(2 * seq, 2)])
    project(seq, 0, OWN, True)
    relay(1)
    send_part(6, 7)
    attend(seq, 0, 0)
    send("ctx", "ctx", ctx_out.at[0, 1 - core], ctx_in.at[SIB], sibling)
    ctx_in[OWN] = ctx_out[0, core]
    relay(2)
    send_part(8)
    send_rest(1, 2)
    relay(3)
    send_rest(3, 4)
    collect(0)
    relay(4)
    relay(5)
    send_rest(5, 6)

    loaded("w", w.at[OWN, pl.ds(0, QKV)])
    loaded("one", gains.at[0])
    loaded("two", gains.at[1])
    loaded("cot", cot)
    arrived("so", w.at[SIB, pl.ds(OUT, 1)])
    collect_sibling(0)
    arrived("ctx", ctx_in.at[pl.ds(1, 3)])
    attn = dot(ctx_in[...].reshape(768, 256), w[:, OUT].reshape(768, 768), 0, 0)
    n1, r1 = norm(x[h].astype(F32) + attn)
    normed_one[...] = n1
    inverse_one[...] = r1
    h1 = n1 * gains[0:1]
    hidden[...] = h1
    hidden_low[...] = h1.astype(BF16)

    def go_up(slot):
        up = dot(hidden_low[...], w[slot, UP : UP + 4].reshape(768, 768))
        phi = 0.5 * (1.0 + lax.erf(up * 0.7071067811865476))
        slope[slot] = phi + up * (0.3989422804014327 * jnp.exp(-0.5 * up * up))
        act[slot] = (up * phi).astype(BF16)

    def go_down(slot):
        return dot(act[slot], w[slot, DOWN : DOWN + 4].reshape(768, 768))

    relay(6)
    send_part(9)
    send_rest(7, 8)
    go_up(OWN)
    relay(7)
    send_part(10)
    arrived("su", w.at[SIB, pl.ds(UP, 4)])
    go_up(SIB)
    relay(8)
    send_part(11)
    send_rest(9, 10, 11)
    arrived("sd", w.at[SIB, pl.ds(DOWN, 4)])
    total[...] = hidden[...] + go_down(OWN) + go_down(SIB)
    collect(1)
    go_up(FAR)
    collect_sibling(1)
    go_up(FARSIB)
    collect(2)
    relay(9)
    collect(3)
    total[...] += go_down(FAR)
    collect_sibling(2)
    collect_sibling(3)
    z2 = total[...] + go_down(FARSIB)

    n2, r2 = norm(z2)
    position = lax.broadcasted_iota(jnp.int32, (256, 1), 0) + 256 * core
    valid = (position < lengths[seq]).astype(F32)
    activations[h] = (valid * (n2 * gains[1:2])).astype(BF16)
    send("rows", "ay", activations.at[h], activations.at[h], across)
    send("rows", "all", activations.at[h], activations.at[h], sibling)
    d_z2 = norm_back(cot[...].astype(F32) * valid * gains[1:2], n2, r2)
    d_z2_low = d_z2.astype(BF16)
    relay(10)

    steps = []
    for slot in range(4):
        d_act = dot(d_z2_low, w[slot, DOWN : DOWN + 4].reshape(768, 768), 1, 1)
        steps.append((d_act * slope[slot]).astype(BF16))
    grad_h1 = d_z2
    for slot in range(4):
        grad_h1 = grad_h1 + dot(steps[slot], w[slot, UP : UP + 4].reshape(768, 768), 1, 1)

    d_z1 = norm_back(grad_h1 * gains[0:1], normed_one[...], inverse_one[...])
    grad_z1[...] = d_z1
    d_ctx = dot(w[:, OUT].reshape(768, 768), d_z1.astype(BF16), 1, 1).astype(BF16)
    dctx_out[...] = d_ctx.reshape(4, 192, 256)
    send("dctx", "dctx", dctx_out.at[SIB], dctx_in.at[core, 0], sibling)
    send("dctx", "dctx", dctx_out.at[FARSIB], dctx_in.at[core, 1], sibling)
    dctx_in[core, 0] = dctx_out[OWN]
    dctx_in[core, 1] = dctx_out[FAR]
    relay(11)
    arrived("dctx", dctx_in.at[1 - core])

    def attend_back(which):
        d_scores = []
        for head in range(3):
            rows = head_rows(0, head)
            d_out = jnp.concatenate([dctx_in[0, which, rows], dctx_in[1, which, rows]], axis=1)
            probability = probs[which, head].astype(F32)
            d_weights = dot(qkv[which, head_rows(2, head)], d_out, 0, 0)
            mean = jnp.sum(probability * d_weights, axis=0, keepdims=True)
            d_scores.append((probability * (d_weights - mean)).astype(BF16))
        for head in range(3):
            rows = head_rows(0, head)
            d_out = jnp.concatenate([dctx_in[0, which, rows], dctx_in[1, which, rows]], axis=1)
            d_query = (0.125 * dot(qkv[which, head_rows(1, head)], d_scores[head])).astype(BF16)
            d_key = 0.125 * dot(d_scores[head], qkv[which, head_rows(0, head)], 1, 1)
            d_value = dot(probs[which, head], d_out, 1, 1)
            pieces = (d_query, d_key.astype(BF16).T, d_value.astype(BF16).T)
            for j, piece in enumerate(pieces):
                for half in range(2):
                    span = slice(256 * half, 256 * half + 256)
                    grad_qkv[which, half, head_rows(j, head)] = piece[:, span]

    def adapter_grads(which):
        for j in range(2):
            rows = slice(384 * j, 384 * j + 192)
            grads[which, j] = 2.0 * (
                dot(low[:, :256], grad_qkv[which, 0, rows], 1, 1)
                + dot(low[:, 256:], grad_qkv[which, 1, rows], 1, 1)
            )

    def batch_start(s):
        send("g", ("g", s), grads.at[0 if s == 0 else 1 + s], grads_in.at[1 + s], batch_peers[s])

    def batch_end(s):
        arrived(("g", s), grads_in.at[1 + s])
        grads[2 + s] = grads[0 if s == 0 else 1 + s] + grads_in[1 + s]

    attend_back(0)
    adapter_grads(0)

    collect(4)
    arrived("b", adapter_up.at[1])
    project(seq, 1, FAR, False)
    attend(seq, 1, None)
    arrived("ay", activations.at[flip(h, 2)])
    send("rows", "all", activations.at[flip(h, 2)], activations.at[flip(h, 2)], sibling)
    attend_back(1)
    adapter_grads(1)
    send("g", "g", grads.at[1], grads_in.at[0], across)

    def adapter_rows(half):
        d_low = 0.0
        for which in range(2):
            d_low = d_low + dot(adapter_up[which].astype(BF16), grad_qkv[which, half, :576])
        d_low = 2.0 * d_low
        coarse = d_low.astype(BF16)
        fine = (d_low - coarse.astype(F32)).astype(BF16)
        grad_qkv[0, half, 576:] = jnp.concatenate([coarse, fine], axis=0)

    def input_part(half, t):
        span = slice(128 * t, 128 * t + 128)
        return dot(grad_qkv[0, half][:, span], adapted(OWN, 608), 0, 0) + dot(
            grad_qkv[1, half, :576][:, span], adapted(FAR, 576), 0, 0
        )

    adapter_rows(1 - core)
    for t in range(2):
        part_out[t] = input_part(1 - core, t).astype(BF16)
        send("rows", ("p", t), part_out.at[t], part_in.at[t], sibling)
    adapter_rows(core)
    for t in range(2):
        span = slice(128 * t, 128 * t + 128)
        own = grad_z1[span] + input_part(core, t)
        arrived(("p", t), part_in.at[t])
        input_grad[h, span] = (own + part_in[t].astype(F32)).astype(BF16)
        for n, (first, count) in enumerate(CHUNKS):
            if first // 128 == t:
                block = input_grad.at[h, pl.ds(first, count)]
                send("rows", ("i", n), block, block, across)
    send("rows", "all", input_grad.at[h], input_grad.at[h], sibling)

    def pass_on(n):
        first, count = CHUNKS[n]
        block = input_grad.at[flip(h, 2), pl.ds(first, count)]
        arrived(("i", n), block)
        send("rows", "all", block, block, sibling)

    arrived("g", grads_in.at[0])
    grads[0] += grads_in[0]
    batch_start(0)
    for s in range(batch_steps):
        batch_end(s)
        if s + 1 < batch_steps:
            batch_start(s + 1)
        if s == 1:
            pass_on(0)
    final = grads[1 + batch_steps]
    grads_out[0] = final[0, 0:8]
    grads_out[1] = final[1, 8:16]
    for n in range(1, len(CHUNKS)):
        pass_on(n)
    arrived("all", activations)

    sent("y", w.at[FAR, pl.ds(0, 3)])
    sent("x", w.at[FAR, pl.ds(0, 3)])
    sent("z", w.at[FAR, pl.ds(0, 3)])
    sent("t", w.at[FAR, pl.ds(0, 3), pl.ds(0, 96)])
    sent("d", w.at[FAR, pl.ds(0, 3), pl.ds(0, 96)])
    sent("c", w.at[FAR, pl.ds(0, 9)])
    sent("w", w.at[SIB, pl.ds(0, 9)])
    sent("ctx", ctx_in.at[pl.ds(0, 3)])
    sent("dctx", dctx_in.at[0])
    sent("rows", w.at[pl.ds(0, 4), pl.ds(0, 7), pl.ds(0, 64)])
    sent("b", adapter_up.at[0])
    sent("g", grads_in)


def hand_over(activations, input_grad, grads, *rest):
    targets, sem = rest[:4], rest[4]
    sources = (activations, input_grad, grads.at[0], grads.at[1])
    copies = [
        pltpu.make_async_copy(source, target, sem.at[n])
        for n, (source, target) in enumerate(zip(sources, targets))
    ]
    for c in copies:
        c.start()
    for c in copies:
        c.wait()


def body(batch_steps, *given):
    (
        tokens,
        lengths,
        w_query,
        w_key,
        w_value,
        w_out,
        down_query,
        down_value,
        up_query,
        up_value,
        w_up,
        w_down,
        gain_attn,
        gain_ffn,
        cotangent,
    ) = given
    anywhere = pl.BlockSpec(memory_space=pl.ANY)
    in_vmem = pl.BlockSpec(memory_space=pltpu.VMEM)
    in_hbm = pl.BlockSpec(memory_space=pltpu.HBM)
    vmem = pltpu.VMEM
    results = pl.pallas_call(
        functools.partial(kernel, batch_steps),
        out_shape=(
            vmem((4, 256, 768), BF16),
            vmem((4, 256, 768), BF16),
            vmem((2, 8, 192), F32),
        ),
        in_specs=[pl.BlockSpec(memory_space=pltpu.SMEM)] + [in_hbm] * 14,
        out_specs=(in_vmem,) * 3,
        scratch_shapes=[
            vmem((4, 256, 768), BF16),
            vmem((4, 13, 192, 768), BF16),
            vmem((2, 8, 768), BF16),
            vmem((2, 8, 192), BF16),
            vmem((2, 768), F32),
            vmem((256, 768), BF16),
            vmem((2, 16, 576), F32),
            vmem((16, 512), BF16),
            vmem((2, 576, 512), BF16),
            vmem((2, 3, 512, 512), BF16),
            vmem((2, 2, 192, 256), BF16),
            vmem((4, 192, 256), BF16),
            vmem((256, 768), F32),
            vmem((256, 1), F32),
            vmem((256, 768), F32),
            vmem((256, 768), BF16),
            vmem((4, 256, 768), BF16),
            vmem((4, 256, 768), F32),
            vmem((256, 768), F32),
            vmem((256, 768), F32),
            vmem((4, 192, 256), BF16),
            vmem((2, 2, 192, 256), BF16),
            vmem((2, 2, 608, 256), BF16),
            vmem((2, 128, 768), BF16),
            vmem((2, 128, 768), BF16),
            vmem((2 + batch_steps, 2, 16, 192), F32),
            vmem((1 + batch_steps, 2, 16, 192), F32),
            pltpu.SemaphoreType.DMA((9,)),
            pltpu.SemaphoreType.DMA((len(SEND_GROUPS),)),
            pltpu.SemaphoreType.DMA((35 + batch_steps,)),
        ],
        compiler_params=pltpu.CompilerParams(
            collective_id=0, has_side_effects=True, vmem_limit_bytes=56 * 1024 * 1024
        ),
        cost_estimate=pl.CostEstimate(
            flops=11_000_000_000, bytes_accessed=20_000_000, transcendentals=4_000_000
        ),
    )(
        lengths,
        tokens.reshape(4, 256, 768),
        w_query.T,
        w_key.T,
        w_value.T,
        w_out.reshape(1, 192, 768),
        w_up.reshape(4, 192, 768),
        w_down.reshape(4, 192, 768),
        down_query.T,
        down_value.T,
        up_query,
        up_value,
        gain_attn,
        gain_ffn,
        cotangent.reshape(4, 256, 768),
    )
    rows = jax.ShapeDtypeStruct((4, 256, 768), BF16)
    small = jax.ShapeDtypeStruct((8, 192), F32)
    activations, input_grad, grad_b_query, grad_b_value = pl.pallas_call(
        hand_over,
        out_shape=(rows, rows, small, small),
        in_specs=[anywhere] * 3,
        out_specs=[in_hbm] * 4,
        scratch_shapes=[pltpu.SemaphoreType.DMA((4,))],
        compiler_params=pltpu.CompilerParams(vmem_limit_bytes=1024 * 1024),
    )(*results)
    return (
        activations.reshape(tokens.shape),
        input_grad.reshape(tokens.shape),
        grad_b_query,
        grad_b_value,
    )


def solution(mesh):
    batch_steps = mesh.shape["batch"].bit_length() - 1
    in_specs = (
        P("batch", None),
        P("batch"),
        P(None, "head"),
        P(None, "head"),
        P(None, "head"),
        P("head", None),
        P(),
        P(),
        P(None, "head"),
        P(None, "head"),
        P(None, "head"),
        P("head", None),
        P(),
        P(),
        P("batch", None),
    )
    out_specs = (P("batch", None), P("batch", None), P(None, "head"), P(None, "head"))
    return jax.shard_map(
        functools.partial(body, batch_steps),
        mesh=mesh,
        in_specs=in_specs,
        out_specs=out_specs,
        check_vma=False,
    )
```

time: 104 us -> 69.4 us (0.67)
  Pallas kernels: 87.5 us -> 68.4 us
  local copies, waits for them, and re-layouts: 15.5 us -> 0 us
    pallas_call x1 -> x2, Pallas kernels: 87.5 us -> 68.4 us  [the longest x1 66.7 us: body(): pl.pallas_call(functools.partial(kernel, batch_steps), out_shape=(vmem((4...]
    unnamed x11 -> x0, local copies, waits for them, and re-layouts: 11.6 us -> none
    reshape x2 -> x0, local copies, waits for them, and re-layouts: 2.58 us -> none  [the longest x1 1.31 us: body(): gain_attn.reshape(1, 768)]
    squeeze x1 -> x0, local copies, waits for them, and re-layouts: 1.32 us -> none  [body(): grad_adapters[1]]
where the time goes in v2:
time: 69.4 us; the launch traced here: 69.2 us
  Pallas kernels  68.4 us (99%)
  between operations  0.81 us (1%)
    pallas_call x1, Pallas kernels, body(): pl.pallas_call(functools.partial(kernel, batch_steps), out_shape=(vmem((4...  66.7 us
    pallas_call x1, Pallas kernels, body(): pl.pallas_call(hand_over, out_shape=(rows, rows, small, small), in_specs=...  1.7 us

profile of v2, /device:TPU:0, one launch (start us, length us, event | category | flops | bytes accessed | tf_op | source)
XLA Modules:
  0.0 69.2 jit_solution(17020924053106267064)
XLA Ops:
  0.6 66.7 %shard_map.174 = (bf16[4,256,768]{2,1,0:T(8,128)(2,1)S(1)}, bf16[4,256,768]{2,1,0:T(8,128)(2,1)S(1)}, f32[2,8,192]{2,1,0:T(8,128)S(1)}) custom-call(s32[2]{0:T(128)} %lengths.1, bf16[4,256,768]{2,1,0:T(8,128)(2,1)} %bitcast.12, bf16[192,768]{1,0:T(8,128)(2,1)} %bitcast.18, bf16[192,768]{1,0:T(8,128)(2,1)} %bitcast.19, bf16[192,768]{1,0:T(8,128)(2,1)} %bitcast.20, ...), custom_call_target="tpu_custom_call" | custom-call | flops 11000000512 | bytes 20000000 | tf_op jit(solution)/shard_map/pallas_call | solution.py:525
  67.4 1.7 %shard_map.175 = (bf16[4,256,768]{2,1,0:T(8,128)(2,1)}, bf16[4,256,768]{2,1,0:T(8,128)(2,1)}, f32[8,192]{1,0:T(8,128)}, f32[8,192]{1,0:T(8,128)}) custom-call(bf16[4,256,768]{2,1,0:T(8,128)(2,1)S(1)} %get-tuple-element.11.activations, bf16[4,256,768]{2,1,0:T(8,128)(2,1)S(1)} %get-tuple-element.12.input_grad, f32[2,8,192]{2,1,0:T(8,128)S(1)} %get-tuple-element.13.grads), custom_call_target="tpu_custom_call" | custom-call | tf_op jit(solution)/shard_map/pallas_call | solution.py:591

commit v3 on v2

--- a/solution.py
+++ b/solution.py
@@ -13,11 +13,14 @@
 MESH = pl.DeviceIdType.MESH
 
 OUT, UP, DOWN, QKV, ADAPTER = 0, 1, 5, 9, 12
+ITEMS = 12
 OWN, SIB, FAR, FARSIB = 0, 1, 2, 3
-OVER_Y = (32, 16) * 6
-GROUPS = ((0, 1), (1, 4), (5, 2), (7, 2), (9, 3))
-CHUNKS = ((0, 128), (128, 64), (192, 64))
-SEND_GROUPS = ("y", "x", "z", "t", "d", "c", "w", "ctx", "dctx", "rows", "b", "g")
+OVER_Y = (16, 0, 0, 0, 0, 32, 32, 32, 32, 32, 32, 32)
+TWICE = (1, 2, 3, 4)
+GROUPS = ((0, 1), (1, 2), (3, 2), (5, 2), (7, 1), (8, 1), (9, 3))
+SPANS = ((0, 128), (128, 256), (384, 384))
+PIECES = ((0, 128), (128, 256), (384, 256), (640, 128))
+SEND_GROUPS = ("y", "x", "z", "t", "d", "c", "w", "ctx", "dctx", "rows", "b", "l", "g")
 
 
 def dot(left, right, left_dim=1, right_dim=0):
@@ -45,7 +48,7 @@
 
 
 def kernel(
-    batch_steps,
+    batch,
     lengths,
     tokens,
     w_query,
@@ -74,6 +77,7 @@
     low,
     qkv,
     probs,
+    log_sum,
     ctx_out,
     ctx_in,
     normed_one,
@@ -84,6 +88,7 @@
     slope,
     total,
     grad_z1,
+    input_sum,
     dctx_out,
     dctx_in,
     grad_qkv,
@@ -91,6 +96,8 @@
     part_in,
     grads,
     grads_in,
+    grads_all,
+    grads_sums,
     local_sem,
     send_sem,
     recv_sem,
@@ -107,10 +114,10 @@
     x_peer = (flip(b, 1), h)
     z_peer = (flip(b, 2), h)
     xz_peer = (flip(flip(b, 1), 2), h)
-    batch_peers = [(flip(b, 1 << s), h) for s in range(batch_steps)]
+    batch_peers = [(flip(b, 1 << s), h) for s in range(2, batch.bit_length() - 1)]
 
     barrier = pltpu.get_barrier_semaphore()
-    peers = [sibling, across, diagonal, xz_peer] + batch_peers
+    peers = [sibling, across, diagonal, x_peer, z_peer, xz_peer] + batch_peers
     for peer in peers:
         pl.semaphore_signal(barrier, inc=1, device_id=peer, device_id_type=MESH)
 
@@ -163,7 +170,7 @@
     load("cot", cotangent.at[h], cot)
 
     far = w.at[FAR]
-    pd = 3 - part
+    px, pz, pd = flip(part, 1), flip(part, 2), 3 - part
     group_of = {}
     for first, count in GROUPS:
         for item in range(first, first + count):
@@ -198,17 +205,30 @@
         for item in items:
             mine = rows_of(far, item, part)
             arrived(("y", item), mine)
+            twice = item in TWICE
             key = ("f", group_of[item])
-            send("x", key, mine, mine, x_peer)
-            send("z", key, mine, mine, z_peer)
-            count = OVER_Y[item]
-            rest = rows_of(far, item, part, count, 48 - count)
-            send("d", key, rest, rest, xz_peer)
+            send("x", ("x", item) if twice else key, mine, mine, x_peer)
+            send("z", ("z", item) if twice else key, mine, mine, z_peer)
+            if not twice:
+                count = OVER_Y[item]
+                rest = rows_of(far, item, part, count, 48 - count)
+                send("d", key, rest, rest, xz_peer)
+
+    def relay_again(*items):
+        for item in items:
+            key = ("f", group_of[item])
+            arrived(("x", item), rows_of(far, item, px))
+            over_x = 32 if item % 2 else 16
+            piece = rows_of(far, item, px, over_x, 48 - over_x)
+            send("z", key, piece, piece, z_peer)
+            arrived(("z", item), rows_of(far, item, pz))
+            piece = rows_of(far, item, pz, 0, over_x)
+            send("x", key, piece, piece, x_peer)
 
     def collect(group):
         first, count = GROUPS[group]
         items = pl.ds(first, count)
-        arrived(("f", first), w.at[FAR, items, pl.ds(0, 144)])
+        arrived(("f", first), w.at[FAR, items, pl.ds(0, 48 if first in TWICE else 144)])
         if first < QKV:
             send("c", ("c", first), w.at[FAR, items], w.at[FARSIB, items], sibling)
 
@@ -217,9 +237,15 @@
         arrived(("c", first), w.at[FARSIB, pl.ds(first, count)])
 
     pl.semaphore_wait(barrier, len(peers))
-    send_part(0, 1)
+    send_part(0)
+    send_part(1)
     send_rest(0)
-    send_part(2, 3, 4, 5)
+    send_part(2)
+    send_part(3)
+    send_part(4)
+    send_part(5)
+    send_part(6)
+    send_part(7)
     send("w", "so", w_out, w.at[SIB, pl.ds(OUT, 1)], sibling)
     send("w", "su", w_up, w.at[SIB, pl.ds(UP, 4)], sibling)
     send("w", "sd", w_down, w.at[SIB, pl.ds(DOWN, 4)], sibling)
@@ -233,7 +259,6 @@
     adapter_up[0, :, :192] = jnp.concatenate([raw_up[0].astype(F32), nothing], axis=0)
     adapter_up[0, :, 192:384] = jnp.zeros((16, 192), F32)
     adapter_up[0, :, 384:] = jnp.concatenate([nothing, raw_up[1].astype(F32)], axis=0)
-    send("b", "b", adapter_up.at[0], adapter_up.at[1], across)
 
     def adapted(slot, count):
         return w[slot, QKV:].reshape(768, 768)[:count]
@@ -253,17 +278,21 @@
     def head_rows(j, head):
         return slice(192 * j + HD * head, 192 * j + HD * (head + 1))
 
-    def attend(rows, which, context):
+    def scores_of(rows, which, head):
         position = lax.broadcasted_iota(jnp.int32, (512, 1), 0)
         bias = jnp.where(position < lengths[rows], 0.0, -1e30)
+        query = qkv[which, head_rows(0, head)] * jnp.asarray(0.125, BF16)
+        return dot(qkv[which, head_rows(1, head)], query, 0, 0) + bias
+
+    def attend(rows, which, context):
         for head in range(3):
-            query = qkv[which, head_rows(0, head)] * jnp.asarray(0.125, BF16)
-            scores = dot(qkv[which, head_rows(1, head)], query, 0, 0) + bias
-            exponent = jnp.exp(scores - jnp.max(scores, axis=0, keepdims=True))
-            weights = exponent * (1.0 / jnp.sum(exponent, axis=0, keepdims=True))
-            probs[which, head] = weights.astype(BF16)
-        if context is None:
-            return
+            scores = scores_of(rows, which, head)
+            top = jnp.max(scores, axis=0, keepdims=True)
+            exponent = jnp.exp(scores - top)
+            amount = jnp.sum(exponent, axis=0, keepdims=True)
+            probs[which, head] = (exponent * (1.0 / amount)).astype(BF16)
+            if which == 1:
+                log_sum[0, head] = top + jnp.log(amount)
         for head in range(3):
             out = dot(qkv[which, head_rows(2, head)], probs[which, head]).astype(BF16)
             ctx_out[context, 0, head_rows(0, head)] = out[:, :256]
@@ -275,23 +304,37 @@
     attend(far_seq, 1, 1)
     send("ctx", "ctx", ctx_out.at[1, core], ctx_in.at[FAR], across)
     send("ctx", "ctx", ctx_out.at[1, 1 - core], ctx_in.at[FARSIB], diagonal)
+    send_part(8)
+    send_rest(5)
+    send_rest(6)
+    send_rest(7)
+    send_rest(8)
+    send_part(9)
+    send_part(10)
+    send_part(11)
+    send_rest(9)
+    send_rest(10)
+    send_rest(11)
+    send("b", "b", adapter_up.at[0], adapter_up.at[1], across)
+    send("l", "l", log_sum.at[0], log_sum.at[1], across)
     relay(0)
     loaded("own", x.at[pl.ds(2 * seq, 2)])
     project(seq, 0, OWN, True)
     relay(1)
-    send_part(6, 7)
     attend(seq, 0, 0)
     send("ctx", "ctx", ctx_out.at[0, 1 - core], ctx_in.at[SIB], sibling)
     ctx_in[OWN] = ctx_out[0, core]
     relay(2)
-    send_part(8)
-    send_rest(1, 2)
     relay(3)
-    send_rest(3, 4)
+    relay_again(1)
+    relay(4)
+    relay_again(2)
+    relay(5)
     collect(0)
-    relay(4)
-    relay(5)
-    send_rest(5, 6)
+    relay_again(3)
+    relay(6)
+    relay_again(4)
+    relay(7)
 
     loaded("w", w.at[OWN, pl.ds(0, QKV)])
     loaded("one", gains.at[0])
@@ -314,33 +357,34 @@
         slope[slot] = phi + up * (0.3989422804014327 * jnp.exp(-0.5 * up * up))
         act[slot] = (up * phi).astype(BF16)
 
-    def go_down(slot):
-        return dot(act[slot], w[slot, DOWN : DOWN + 4].reshape(768, 768))
-
-    relay(6)
-    send_part(9)
-    send_rest(7, 8)
+    def go_down(slot, first=0, count=4):
+        rows = slice(192 * first, 192 * (first + count))
+        weights = w[slot, DOWN + first : DOWN + first + count].reshape(192 * count, 768)
+        return dot(act[slot, :, rows], weights)
+
     go_up(OWN)
-    relay(7)
-    send_part(10)
     arrived("su", w.at[SIB, pl.ds(UP, 4)])
     go_up(SIB)
-    relay(8)
-    send_part(11)
-    send_rest(9, 10, 11)
     arrived("sd", w.at[SIB, pl.ds(DOWN, 4)])
     total[...] = hidden[...] + go_down(OWN) + go_down(SIB)
+    relay(8)
     collect(1)
+    collect(2)
     go_up(FAR)
     collect_sibling(1)
+    collect_sibling(2)
     go_up(FARSIB)
-    collect(2)
+    collect(3)
+    collect(4)
+    collect(5)
+    total[...] += go_down(FAR, 0, 3)
+    collect_sibling(3)
+    collect_sibling(4)
+    total[...] += go_down(FARSIB, 0, 3)
+    total[...] += go_down(FAR, 3, 1)
     relay(9)
-    collect(3)
-    total[...] += go_down(FAR)
-    collect_sibling(2)
-    collect_sibling(3)
-    z2 = total[...] + go_down(FARSIB)
+    collect_sibling(5)
+    z2 = total[...] + go_down(FARSIB, 3, 1)
 
     n2, r2 = norm(z2)
     position = lax.broadcasted_iota(jnp.int32, (256, 1), 0) + 256 * core
@@ -362,13 +406,21 @@
 
     d_z1 = norm_back(grad_h1 * gains[0:1], normed_one[...], inverse_one[...])
     grad_z1[...] = d_z1
-    d_ctx = dot(w[:, OUT].reshape(768, 768), d_z1.astype(BF16), 1, 1).astype(BF16)
-    dctx_out[...] = d_ctx.reshape(4, 192, 256)
+    d_z1_low = d_z1.astype(BF16)
+    relay(11)
+
+    def d_context(first):
+        pair = [w[first, OUT], w[first + 2, OUT]]
+        d_ctx = dot(jnp.concatenate(pair, axis=0), d_z1_low, 1, 1).astype(BF16)
+        dctx_out[first] = d_ctx[:192]
+        dctx_out[first + 2] = d_ctx[192:]
+
+    d_context(SIB)
     send("dctx", "dctx", dctx_out.at[SIB], dctx_in.at[core, 0], sibling)
     send("dctx", "dctx", dctx_out.at[FARSIB], dctx_in.at[core, 1], sibling)
+    d_context(OWN)
     dctx_in[core, 0] = dctx_out[OWN]
     dctx_in[core, 1] = dctx_out[FAR]
-    relay(11)
     arrived("dctx", dctx_in.at[1 - core])
 
     def attend_back(which):
@@ -376,7 +428,11 @@
         for head in range(3):
             rows = head_rows(0, head)
             d_out = jnp.concatenate([dctx_in[0, which, rows], dctx_in[1, which, rows]], axis=1)
-            probability = probs[which, head].astype(F32)
+            if which == 0:
+                probability = probs[0, head].astype(F32)
+            else:
+                probability = jnp.exp(scores_of(seq, 1, head) - log_sum[1, head])
+                probs[1, head] = probability.astype(BF16)
             d_weights = dot(qkv[which, head_rows(2, head)], d_out, 0, 0)
             mean = jnp.sum(probability * d_weights, axis=0, keepdims=True)
             d_scores.append((probability * (d_weights - mean)).astype(BF16))
@@ -388,103 +444,104 @@
             d_value = dot(probs[which, head], d_out, 1, 1)
             pieces = (d_query, d_key.astype(BF16).T, d_value.astype(BF16).T)
             for j, piece in enumerate(pieces):
-                for half in range(2):
-                    span = slice(256 * half, 256 * half + 256)
-                    grad_qkv[which, half, head_rows(j, head)] = piece[:, span]
+                grad_qkv[which, head_rows(j, head)] = piece
 
     def adapter_grads(which):
         for j in range(2):
             rows = slice(384 * j, 384 * j + 192)
-            grads[which, j] = 2.0 * (
-                dot(low[:, :256], grad_qkv[which, 0, rows], 1, 1)
-                + dot(low[:, 256:], grad_qkv[which, 1, rows], 1, 1)
-            )
-
-    def batch_start(s):
-        send("g", ("g", s), grads.at[0 if s == 0 else 1 + s], grads_in.at[1 + s], batch_peers[s])
-
-    def batch_end(s):
-        arrived(("g", s), grads_in.at[1 + s])
-        grads[2 + s] = grads[0 if s == 0 else 1 + s] + grads_in[1 + s]
+            both = dot(low[...], grad_qkv[which, rows], 1, 1)
+            grads[which, j] = 2.0 * both[8 * j : 8 * j + 8]
+
+    def adapter_rows(which):
+        d_low = 2.0 * dot(adapter_up[which].astype(BF16), grad_qkv[which, :576])
+        coarse = d_low.astype(BF16)
+        fine = (d_low - coarse.astype(F32)).astype(BF16)
+        grad_qkv[which, 576:] = jnp.concatenate([coarse, fine], axis=0)
+
+    def input_part(which, columns, half=None):
+        weights = w[OWN if which == 0 else FAR, QKV:].reshape(768, 768)[:608, columns]
+        if half is None:
+            return dot(grad_qkv[which], weights, 0, 0).reshape(2, 256, 768)
+        rows = pl.ds(pl.multiple_of(256 * half, 256), 256)
+        return dot(grad_qkv[which, :, rows], weights, 0, 0)
 
     attend_back(0)
+    adapter_rows(0)
+    input_sum[...] = input_part(0, slice(0, 768))
+    input_sum[core] += grad_z1[...]
     adapter_grads(0)
 
-    collect(4)
+    collect(6)
     arrived("b", adapter_up.at[1])
+    arrived("l", log_sum.at[1])
     project(seq, 1, FAR, False)
-    attend(seq, 1, None)
+    attend_back(1)
+    adapter_rows(1)
+    spans = [(t, slice(first, first + count)) for t, (first, count) in enumerate(SPANS)]
+    pieces = [(n, slice(first, first + count)) for n, (first, count) in enumerate(PIECES)]
+    for t, columns in spans:
+        given = input_sum[1 - core, :, columns] + input_part(1, columns, 1 - core)
+        part_out[:, columns] = given.astype(BF16)
+        send("rows", ("p", t), part_out.at[:, columns], part_in.at[:, columns], sibling)
+        if t == 0:
+            adapter_grads(1)
+            send("g", "g", grads.at[1], grads_in, across)
+    for t, columns in spans:
+        own = input_sum[core, :, columns] + input_part(1, columns, core)
+        arrived(("p", t), part_in.at[:, columns])
+        input_grad[h, :, columns] = (own + part_in[:, columns].astype(F32)).astype(BF16)
+        for n, piece in pieces:
+            if columns.start <= piece.start < columns.stop:
+                block = input_grad.at[h, :, piece]
+                send("rows", ("i", n), block, block, across)
+    send("rows", "all", input_grad.at[h], input_grad.at[h], sibling)
+
+    def pass_on(n):
+        block = input_grad.at[flip(h, 2), :, pieces[n][1]]
+        arrived(("i", n), block)
+        send("rows", "all", block, block, sibling)
+
     arrived("ay", activations.at[flip(h, 2)])
     send("rows", "all", activations.at[flip(h, 2)], activations.at[flip(h, 2)], sibling)
-    attend_back(1)
-    adapter_grads(1)
-    send("g", "g", grads.at[1], grads_in.at[0], across)
-
-    def adapter_rows(half):
-        d_low = 0.0
-        for which in range(2):
-            d_low = d_low + dot(adapter_up[which].astype(BF16), grad_qkv[which, half, :576])
-        d_low = 2.0 * d_low
-        coarse = d_low.astype(BF16)
-        fine = (d_low - coarse.astype(F32)).astype(BF16)
-        grad_qkv[0, half, 576:] = jnp.concatenate([coarse, fine], axis=0)
-
-    def input_part(half, t):
-        span = slice(128 * t, 128 * t + 128)
-        return dot(grad_qkv[0, half][:, span], adapted(OWN, 608), 0, 0) + dot(
-            grad_qkv[1, half, :576][:, span], adapted(FAR, 576), 0, 0
-        )
-
-    adapter_rows(1 - core)
-    for t in range(2):
-        part_out[t] = input_part(1 - core, t).astype(BF16)
-        send("rows", ("p", t), part_out.at[t], part_in.at[t], sibling)
-    adapter_rows(core)
-    for t in range(2):
-        span = slice(128 * t, 128 * t + 128)
-        own = grad_z1[span] + input_part(core, t)
-        arrived(("p", t), part_in.at[t])
-        input_grad[h, span] = (own + part_in[t].astype(F32)).astype(BF16)
-        for n, (first, count) in enumerate(CHUNKS):
-            if first // 128 == t:
-                block = input_grad.at[h, pl.ds(first, count)]
-                send("rows", ("i", n), block, block, across)
-    send("rows", "all", input_grad.at[h], input_grad.at[h], sibling)
-
-    def pass_on(n):
-        first, count = CHUNKS[n]
-        block = input_grad.at[flip(h, 2), pl.ds(first, count)]
-        arrived(("i", n), block)
-        send("rows", "all", block, block, sibling)
-
-    arrived("g", grads_in.at[0])
-    grads[0] += grads_in[0]
-    batch_start(0)
-    for s in range(batch_steps):
-        batch_end(s)
-        if s + 1 < batch_steps:
-            batch_start(s + 1)
-        if s == 1:
-            pass_on(0)
-    final = grads[1 + batch_steps]
-    grads_out[0] = final[0, 0:8]
-    grads_out[1] = final[1, 8:16]
-    for n in range(1, len(CHUNKS)):
+    arrived("g", grads_in)
+    grads_all[part] = grads[0] + grads_in[...]
+    for peer in (x_peer, z_peer, xz_peer):
+        send("g", "sums", grads_all.at[part], grads_all.at[part], peer)
+    pass_on(0)
+    arrived("sums", grads_all.at[pl.ds(0, 3)])
+    sums = (grads_all[0] + grads_all[1]) + (grads_all[2] + grads_all[3])
+    for n, peer in enumerate(batch_peers):
+        grads_sums[2 * n] = sums
+        send("g", ("g", n), grads_sums.at[2 * n], grads_sums.at[2 * n + 1], peer)
+        if n == 0:
+            for m in range(1, len(pieces)):
+                pass_on(m)
+        arrived(("g", n), grads_sums.at[2 * n + 1])
+        sums = sums + grads_sums[2 * n + 1]
+    grads_out[...] = sums
+    for n in range(1, 1 if batch_peers else len(pieces)):
         pass_on(n)
     arrived("all", activations)
 
+    def rows_block(count):
+        tiles = count // 16
+        shapes = [(m, n, tiles // (m * n)) for m in (1, 2, 3, 4) for n in range(1, 13) if tiles % (m * n) == 0]
+        inner, outer, depth = next(shape for shape in shapes if shape[2] <= 12)
+        return w.at[pl.ds(0, inner), pl.ds(0, outer), pl.ds(0, 16 * depth)]
+
     sent("y", w.at[FAR, pl.ds(0, 3)])
-    sent("x", w.at[FAR, pl.ds(0, 3)])
-    sent("z", w.at[FAR, pl.ds(0, 3)])
-    sent("t", w.at[FAR, pl.ds(0, 3), pl.ds(0, 96)])
-    sent("d", w.at[FAR, pl.ds(0, 3), pl.ds(0, 96)])
+    sent("x", rows_block(48 * ITEMS + 24 * len(TWICE)))
+    sent("z", rows_block(48 * ITEMS + 24 * len(TWICE)))
+    sent("t", rows_block(sum(OVER_Y)))
+    sent("d", rows_block(sum(48 - OVER_Y[n] for n in range(ITEMS) if n not in TWICE)))
     sent("c", w.at[FAR, pl.ds(0, 9)])
     sent("w", w.at[SIB, pl.ds(0, 9)])
     sent("ctx", ctx_in.at[pl.ds(0, 3)])
     sent("dctx", dctx_in.at[0])
     sent("rows", w.at[pl.ds(0, 4), pl.ds(0, 7), pl.ds(0, 64)])
     sent("b", adapter_up.at[0])
-    sent("g", grads_in)
+    sent("l", log_sum.at[0])
+    sent("g", grads_sums.at[pl.ds(0, 4 + len(batch_peers))])
 
 
 def hand_over(activations, input_grad, grads, *rest):
@@ -500,7 +557,7 @@
         c.wait()
 
 
-def body(batch_steps, *given):
+def body(batch, *given):
     (
         tokens,
         lengths,
@@ -523,7 +580,7 @@
     in_hbm = pl.BlockSpec(memory_space=pltpu.HBM)
     vmem = pltpu.VMEM
     results = pl.pallas_call(
-        functools.partial(kernel, batch_steps),
+        functools.partial(kernel, batch),
         out_shape=(
             vmem((4, 256, 768), BF16),
             vmem((4, 256, 768), BF16),
@@ -542,6 +599,7 @@
             vmem((16, 512), BF16),
             vmem((2, 576, 512), BF16),
             vmem((2, 3, 512, 512), BF16),
+            vmem((2, 3, 1, 512), F32),
             vmem((2, 2, 192, 256), BF16),
             vmem((4, 192, 256), BF16),
             vmem((256, 768), F32),
@@ -552,16 +610,19 @@
             vmem((4, 256, 768), F32),
             vmem((256, 768), F32),
             vmem((256, 768), F32),
+            vmem((2, 256, 768), F32),
             vmem((4, 192, 256), BF16),
             vmem((2, 2, 192, 256), BF16),
-            vmem((2, 2, 608, 256), BF16),
-            vmem((2, 128, 768), BF16),
-            vmem((2, 128, 768), BF16),
-            vmem((2 + batch_steps, 2, 16, 192), F32),
-            vmem((1 + batch_steps, 2, 16, 192), F32),
+            vmem((2, 608, 512), BF16),
+            vmem((256, 768), BF16),
+            vmem((256, 768), BF16),
+            vmem((2, 2, 8, 192), F32),
+            vmem((2, 8, 192), F32),
+            vmem((4, 2, 8, 192), F32),
+            vmem((2 * batch.bit_length(), 2, 8, 192), F32),
             pltpu.SemaphoreType.DMA((9,)),
             pltpu.SemaphoreType.DMA((len(SEND_GROUPS),)),
-            pltpu.SemaphoreType.DMA((35 + batch_steps,)),
+            pltpu.SemaphoreType.DMA((36 + 2 * len(TWICE) + batch.bit_length() + len(SPANS) + len(PIECES),)),
         ],
         compiler_params=pltpu.CompilerParams(
             collective_id=0, has_side_effects=True, vmem_limit_bytes=56 * 1024 * 1024
@@ -605,7 +666,7 @@
 
 
 def solution(mesh):
-    batch_steps = mesh.shape["batch"].bit_length() - 1
+    batch = mesh.shape["batch"]
     in_specs = (
         P("batch", None),
         P("batch"),
@@ -625,7 +686,7 @@
     )
     out_specs = (P("batch", None), P("batch", None), P(None, "head"), P(None, "head"))
     return jax.shard_map(
-        functools.partial(body, batch_steps),
+        functools.partial(body, batch),
         mesh=mesh,
         in_specs=in_specs,
         out_specs=out_specs,

time: 69.4 us -> 62.3 us (0.90)
  Pallas kernels: 68.4 us -> 61.4 us
    pallas_call x1, Pallas kernels: 66.7 us -> 59.7 us  [body(): pl.pallas_call(functools.partial(kernel, batch), out_shape=(vmem((4, 256,...]
where the time goes in v3:
time: 62.3 us; the launch traced here: 62.2 us
  Pallas kernels  61.4 us (99%)
  between operations  0.81 us (1%)
    pallas_call x1, Pallas kernels, body(): pl.pallas_call(functools.partial(kernel, batch), out_shape=(vmem((4, 256,...  59.7 us
    pallas_call x1, Pallas kernels, body(): pl.pallas_call(hand_over, out_shape=(rows, rows, small, small), in_specs=...  1.7 us

profile of v3, /device:TPU:0, one launch (start us, length us, event | category | flops | bytes accessed | tf_op | source)
XLA Modules:
  0.0 62.2 jit_solution(6132308087866970981)
XLA Ops:
  0.6 59.7 %shard_map.174 = (bf16[4,256,768]{2,1,0:T(8,128)(2,1)S(1)}, bf16[4,256,768]{2,1,0:T(8,128)(2,1)S(1)}, f32[2,8,192]{2,1,0:T(8,128)S(1)}) custom-call(s32[2]{0:T(128)} %lengths.1, bf16[4,256,768]{2,1,0:T(8,128)(2,1)} %bitcast.12, bf16[192,768]{1,0:T(8,128)(2,1)} %bitcast.18, bf16[192,768]{1,0:T(8,128)(2,1)} %bitcast.19, bf16[192,768]{1,0:T(8,128)(2,1)} %bitcast.20, ...), custom_call_target="tpu_custom_call" | custom-call | flops 11000000512 | bytes 20000000 | tf_op jit(solution)/shard_map/pallas_call | solution.py:582
  60.3 1.7 %shard_map.175 = (bf16[4,256,768]{2,1,0:T(8,128)(2,1)}, bf16[4,256,768]{2,1,0:T(8,128)(2,1)}, f32[8,192]{1,0:T(8,128)}, f32[8,192]{1,0:T(8,128)}) custom-call(bf16[4,256,768]{2,1,0:T(8,128)(2,1)S(1)} %get-tuple-element.11.activations, bf16[4,256,768]{2,1,0:T(8,128)(2,1)S(1)} %get-tuple-element.12.input_grad, f32[2,8,192]{2,1,0:T(8,128)S(1)} %get-tuple-element.13.grads), custom_call_target="tpu_custom_call" | custom-call | tf_op jit(solution)/shard_map/pallas_call | solution.py:652

commit v4 on v3

--- a/solution.py
+++ b/solution.py
@@ -19,7 +19,13 @@
 TWICE = (1, 2, 3, 4)
 GROUPS = ((0, 1), (1, 2), (3, 2), (5, 2), (7, 1), (8, 1), (9, 3))
 SPANS = ((0, 128), (128, 256), (384, 384))
-PIECES = ((0, 128), (128, 256), (384, 256), (640, 128))
+PIECES = (
+    (0, 256, 0, 128),
+    (0, 256, 128, 256),
+    (0, 256, 384, 256),
+    (0, 128, 640, 128),
+    (128, 128, 640, 128),
+)
 SEND_GROUPS = ("y", "x", "z", "t", "d", "c", "w", "ctx", "dctx", "rows", "b", "l", "g")
 
 
@@ -245,7 +251,7 @@
     send_part(4)
     send_part(5)
     send_part(6)
-    send_part(7)
+    pl.when(core == 1)(lambda: send_part(7))
     send("w", "so", w_out, w.at[SIB, pl.ds(OUT, 1)], sibling)
     send("w", "su", w_up, w.at[SIB, pl.ds(UP, 4)], sibling)
     send("w", "sd", w_down, w.at[SIB, pl.ds(DOWN, 4)], sibling)
@@ -304,6 +310,7 @@
     attend(far_seq, 1, 1)
     send("ctx", "ctx", ctx_out.at[1, core], ctx_in.at[FAR], across)
     send("ctx", "ctx", ctx_out.at[1, 1 - core], ctx_in.at[FARSIB], diagonal)
+    pl.when(core == 0)(lambda: send_part(7))
     send_part(8)
     send_rest(5)
     send_rest(6)
@@ -334,7 +341,7 @@
     relay_again(3)
     relay(6)
     relay_again(4)
-    relay(7)
+    pl.when(core == 1)(lambda: relay(7))
 
     loaded("w", w.at[OWN, pl.ds(0, QKV)])
     loaded("one", gains.at[0])
@@ -362,12 +369,14 @@
         weights = w[slot, DOWN + first : DOWN + first + count].reshape(192 * count, 768)
         return dot(act[slot, :, rows], weights)
 
+    pl.when(core == 1)(lambda: relay(8))
     go_up(OWN)
+    pl.when(core == 0)(lambda: relay(7))
     arrived("su", w.at[SIB, pl.ds(UP, 4)])
     go_up(SIB)
     arrived("sd", w.at[SIB, pl.ds(DOWN, 4)])
     total[...] = hidden[...] + go_down(OWN) + go_down(SIB)
-    relay(8)
+    pl.when(core == 0)(lambda: relay(8))
     collect(1)
     collect(2)
     go_up(FAR)
@@ -400,6 +409,7 @@
     for slot in range(4):
         d_act = dot(d_z2_low, w[slot, DOWN : DOWN + 4].reshape(768, 768), 1, 1)
         steps.append((d_act * slope[slot]).astype(BF16))
+    relay(11)
     grad_h1 = d_z2
     for slot in range(4):
         grad_h1 = grad_h1 + dot(steps[slot], w[slot, UP : UP + 4].reshape(768, 768), 1, 1)
@@ -407,7 +417,6 @@
     d_z1 = norm_back(grad_h1 * gains[0:1], normed_one[...], inverse_one[...])
     grad_z1[...] = d_z1
     d_z1_low = d_z1.astype(BF16)
-    relay(11)
 
     def d_context(first):
         pair = [w[first, OUT], w[first + 2, OUT]]
@@ -478,7 +487,6 @@
     attend_back(1)
     adapter_rows(1)
     spans = [(t, slice(first, first + count)) for t, (first, count) in enumerate(SPANS)]
-    pieces = [(n, slice(first, first + count)) for n, (first, count) in enumerate(PIECES)]
     for t, columns in spans:
         given = input_sum[1 - core, :, columns] + input_part(1, columns, 1 - core)
         part_out[:, columns] = given.astype(BF16)
@@ -486,20 +494,27 @@
         if t == 0:
             adapter_grads(1)
             send("g", "g", grads.at[1], grads_in, across)
+    def piece_of(rows, n):
+        row, count, column, width = PIECES[n]
+        return input_grad.at[rows, pl.ds(row, count), pl.ds(column, width)]
+
     for t, columns in spans:
         own = input_sum[core, :, columns] + input_part(1, columns, core)
         arrived(("p", t), part_in.at[:, columns])
         input_grad[h, :, columns] = (own + part_in[:, columns].astype(F32)).astype(BF16)
-        for n, piece in pieces:
-            if columns.start <= piece.start < columns.stop:
-                block = input_grad.at[h, :, piece]
+        for n, (row, rows, column, width) in enumerate(PIECES):
+            if columns.start <= column < columns.stop:
+                block = piece_of(h, n)
                 send("rows", ("i", n), block, block, across)
+                if n == len(PIECES) - 1:
+                    send("rows", "all", block, block, diagonal)
     send("rows", "all", input_grad.at[h], input_grad.at[h], sibling)
 
     def pass_on(n):
-        block = input_grad.at[flip(h, 2), :, pieces[n][1]]
+        block = piece_of(flip(h, 2), n)
         arrived(("i", n), block)
-        send("rows", "all", block, block, sibling)
+        if n < len(PIECES) - 1:
+            send("rows", "all", block, block, sibling)
 
     arrived("ay", activations.at[flip(h, 2)])
     send("rows", "all", activations.at[flip(h, 2)], activations.at[flip(h, 2)], sibling)
@@ -514,12 +529,12 @@
         grads_sums[2 * n] = sums
         send("g", ("g", n), grads_sums.at[2 * n], grads_sums.at[2 * n + 1], peer)
         if n == 0:
-            for m in range(1, len(pieces)):
+            for m in range(1, len(PIECES)):
                 pass_on(m)
         arrived(("g", n), grads_sums.at[2 * n + 1])
         sums = sums + grads_sums[2 * n + 1]
     grads_out[...] = sums
-    for n in range(1, 1 if batch_peers else len(pieces)):
+    for n in range(1, 1 if batch_peers else len(PIECES)):
         pass_on(n)
     arrived("all", activations)
 

time: 62.3 us -> 61.6 us (0.989)
  Pallas kernels: 61.4 us -> 60.7 us
    pallas_call x1, Pallas kernels: 59.7 us -> 59 us  [body(): pl.pallas_call(functools.partial(kernel, batch), out_shape=(vmem((4, 256,...]
where the time goes in v4:
time: 61.6 us; the launch traced here: 61.5 us
  Pallas kernels  60.7 us (99%)
  between operations  0.81 us (1%)
    pallas_call x1, Pallas kernels, body(): pl.pallas_call(functools.partial(kernel, batch), out_shape=(vmem((4, 256,...  59 us
    pallas_call x1, Pallas kernels, body(): pl.pallas_call(hand_over, out_shape=(rows, rows, small, small), in_specs=...  1.7 us

profile of v4, /device:TPU:0, one launch (start us, length us, event | category | flops | bytes accessed | tf_op | source)
XLA Modules:
  0.0 61.5 jit_solution(1966394643725929595)
XLA Ops:
  0.6 59.0 %shard_map.174 = (bf16[4,256,768]{2,1,0:T(8,128)(2,1)S(1)}, bf16[4,256,768]{2,1,0:T(8,128)(2,1)S(1)}, f32[2,8,192]{2,1,0:T(8,128)S(1)}) custom-call(s32[2]{0:T(128)} %lengths.1, bf16[4,256,768]{2,1,0:T(8,128)(2,1)} %bitcast.12, bf16[192,768]{1,0:T(8,128)(2,1)} %bitcast.18, bf16[192,768]{1,0:T(8,128)(2,1)} %bitcast.19, bf16[192,768]{1,0:T(8,128)(2,1)} %bitcast.20, ...), custom_call_target="tpu_custom_call" | custom-call | flops 11000000512 | bytes 20000000 | tf_op jit(solution)/shard_map/pallas_call | solution.py:597
  59.6 1.7 %shard_map.175 = (bf16[4,256,768]{2,1,0:T(8,128)(2,1)}, bf16[4,256,768]{2,1,0:T(8,128)(2,1)}, f32[8,192]{1,0:T(8,128)}, f32[8,192]{1,0:T(8,128)}) custom-call(bf16[4,256,768]{2,1,0:T(8,128)(2,1)S(1)} %get-tuple-element.11.activations, bf16[4,256,768]{2,1,0:T(8,128)(2,1)S(1)} %get-tuple-element.12.input_grad, f32[2,8,192]{2,1,0:T(8,128)S(1)} %get-tuple-element.13.grads), custom_call_target="tpu_custom_call" | custom-call | tf_op jit(solution)/shard_map/pallas_call | solution.py:667

commit v5 on v4

--- a/solution.py
+++ b/solution.py
@@ -80,6 +80,7 @@
     gains,
     cot,
     adapter_up,
+    ups_out,
     low,
     qkv,
     probs,
@@ -261,10 +262,16 @@
     downs = jnp.concatenate([raw_down[0].astype(F32), raw_down[1].astype(F32)] * 2, axis=0)
     w[OWN, ADAPTER, :32] = downs.astype(BF16)
     w[FAR, ADAPTER, :32] = downs.astype(BF16)
-    nothing = jnp.zeros((8, 192), F32)
-    adapter_up[0, :, :192] = jnp.concatenate([raw_up[0].astype(F32), nothing], axis=0)
-    adapter_up[0, :, 192:384] = jnp.zeros((16, 192), F32)
-    adapter_up[0, :, 384:] = jnp.concatenate([nothing, raw_up[1].astype(F32)], axis=0)
+    ups_out[0] = jnp.concatenate([raw_up[0].astype(F32), raw_up[1].astype(F32)], axis=0).astype(BF16)
+    mine_up = lax.broadcasted_iota(jnp.int32, (16, 192), 0) < 8
+
+    def spread_up(which):
+        both = ups_out[which].astype(F32)
+        adapter_up[which, :, :192] = jnp.where(mine_up, both, 0.0)
+        adapter_up[which, :, 192:384] = jnp.zeros((16, 192), F32)
+        adapter_up[which, :, 384:] = jnp.where(mine_up, 0.0, both)
+
+    spread_up(0)
 
     def adapted(slot, count):
         return w[slot, QKV:].reshape(768, 768)[:count]
@@ -322,7 +329,7 @@
     send_rest(9)
     send_rest(10)
     send_rest(11)
-    send("b", "b", adapter_up.at[0], adapter_up.at[1], across)
+    send("b", "b", ups_out.at[0], ups_out.at[1], across)
     send("l", "l", log_sum.at[0], log_sum.at[1], across)
     relay(0)
     loaded("own", x.at[pl.ds(2 * seq, 2)])
@@ -409,7 +416,6 @@
     for slot in range(4):
         d_act = dot(d_z2_low, w[slot, DOWN : DOWN + 4].reshape(768, 768), 1, 1)
         steps.append((d_act * slope[slot]).astype(BF16))
-    relay(11)
     grad_h1 = d_z2
     for slot in range(4):
         grad_h1 = grad_h1 + dot(steps[slot], w[slot, UP : UP + 4].reshape(768, 768), 1, 1)
@@ -417,6 +423,7 @@
     d_z1 = norm_back(grad_h1 * gains[0:1], normed_one[...], inverse_one[...])
     grad_z1[...] = d_z1
     d_z1_low = d_z1.astype(BF16)
+    relay(11)
 
     def d_context(first):
         pair = [w[first, OUT], w[first + 2, OUT]]
@@ -481,24 +488,25 @@
     adapter_grads(0)
 
     collect(6)
-    arrived("b", adapter_up.at[1])
+    arrived("b", ups_out.at[1])
+    spread_up(1)
     arrived("l", log_sum.at[1])
     project(seq, 1, FAR, False)
     attend_back(1)
     adapter_rows(1)
     spans = [(t, slice(first, first + count)) for t, (first, count) in enumerate(SPANS)]
-    for t, columns in spans:
+    def piece_of(rows, n):
+        row, count, column, width = PIECES[n]
+        return input_grad.at[rows, pl.ds(row, count), pl.ds(column, width)]
+
+    def give(t):
+        columns = spans[t][1]
         given = input_sum[1 - core, :, columns] + input_part(1, columns, 1 - core)
         part_out[:, columns] = given.astype(BF16)
         send("rows", ("p", t), part_out.at[:, columns], part_in.at[:, columns], sibling)
-        if t == 0:
-            adapter_grads(1)
-            send("g", "g", grads.at[1], grads_in, across)
-    def piece_of(rows, n):
-        row, count, column, width = PIECES[n]
-        return input_grad.at[rows, pl.ds(row, count), pl.ds(column, width)]
-
-    for t, columns in spans:
+
+    def take(t):
+        columns = spans[t][1]
         own = input_sum[core, :, columns] + input_part(1, columns, core)
         arrived(("p", t), part_in.at[:, columns])
         input_grad[h, :, columns] = (own + part_in[:, columns].astype(F32)).astype(BF16)
@@ -508,6 +516,15 @@
                 send("rows", ("i", n), block, block, across)
                 if n == len(PIECES) - 1:
                     send("rows", "all", block, block, diagonal)
+
+    give(0)
+    adapter_grads(1)
+    send("g", "g", grads.at[1], grads_in, across)
+    give(1)
+    take(0)
+    give(2)
+    take(1)
+    take(2)
     send("rows", "all", input_grad.at[h], input_grad.at[h], sibling)
 
     def pass_on(n):
@@ -554,7 +571,7 @@
     sent("ctx", ctx_in.at[pl.ds(0, 3)])
     sent("dctx", dctx_in.at[0])
     sent("rows", w.at[pl.ds(0, 4), pl.ds(0, 7), pl.ds(0, 64)])
-    sent("b", adapter_up.at[0])
+    sent("b", ups_out.at[0])
     sent("l", log_sum.at[0])
     sent("g", grads_sums.at[pl.ds(0, 4 + len(batch_peers))])
 
@@ -611,6 +628,7 @@
             vmem((2, 768), F32),
             vmem((256, 768), BF16),
             vmem((2, 16, 576), F32),
+            vmem((2, 16, 192), BF16),
             vmem((16, 512), BF16),
             vmem((2, 576, 512), BF16),
             vmem((2, 3, 512, 512), BF16),
@@ -637,7 +655,7 @@
             vmem((2 * batch.bit_length(), 2, 8, 192), F32),
             pltpu.SemaphoreType.DMA((9,)),
             pltpu.SemaphoreType.DMA((len(SEND_GROUPS),)),
-            pltpu.SemaphoreType.DMA((36 + 2 * len(TWICE) + batch.bit_length() + len(SPANS) + len(PIECES),)),
+            pltpu.SemaphoreType.DMA((33 + 2 * len(TWICE) + batch.bit_length() + len(SPANS) + len(PIECES),)),
         ],
         compiler_params=pltpu.CompilerParams(
             collective_id=0, has_side_effects=True, vmem_limit_bytes=56 * 1024 * 1024

time: 61.6 us -> 61.1 us (level)
  no operation moved by 1% of the time
where the time goes in v5:
time: 61.1 us; the launch traced here: 61 us
  Pallas kernels  60.1 us (98%)
  between operations  0.81 us (1%)
    pallas_call x1, Pallas kernels, body(): pl.pallas_call(functools.partial(kernel, batch), out_shape=(vmem((4, 256,...  58.4 us
    pallas_call x1, Pallas kernels, body(): pl.pallas_call(hand_over, out_shape=(rows, rows, small, small), in_specs=...  1.7 us

profile of v5, /device:TPU:0, one launch (start us, length us, event | category | flops | bytes accessed | tf_op | source)
XLA Modules:
  0.0 61.0 jit_solution(9825693320726469514)
XLA Ops:
  0.6 58.4 %shard_map.174 = (bf16[4,256,768]{2,1,0:T(8,128)(2,1)S(1)}, bf16[4,256,768]{2,1,0:T(8,128)(2,1)S(1)}, f32[2,8,192]{2,1,0:T(8,128)S(1)}) custom-call(s32[2]{0:T(128)} %lengths.1, bf16[4,256,768]{2,1,0:T(8,128)(2,1)} %bitcast.12, bf16[192,768]{1,0:T(8,128)(2,1)} %bitcast.18, bf16[192,768]{1,0:T(8,128)(2,1)} %bitcast.19, bf16[192,768]{1,0:T(8,128)(2,1)} %bitcast.20, ...), custom_call_target="tpu_custom_call" | custom-call | flops 11000000512 | bytes 20000000 | tf_op jit(solution)/shard_map/pallas_call | solution.py:614
  59.1 1.7 %shard_map.175 = (bf16[4,256,768]{2,1,0:T(8,128)(2,1)}, bf16[4,256,768]{2,1,0:T(8,128)(2,1)}, f32[8,192]{1,0:T(8,128)}, f32[8,192]{1,0:T(8,128)}) custom-call(bf16[4,256,768]{2,1,0:T(8,128)(2,1)S(1)} %get-tuple-element.11.activations, bf16[4,256,768]{2,1,0:T(8,128)(2,1)S(1)} %get-tuple-element.12.input_grad, f32[2,8,192]{2,1,0:T(8,128)S(1)} %get-tuple-element.13.grads), custom_call_target="tpu_custom_call" | custom-call | tf_op jit(solution)/shard_map/pallas_call | solution.py:685

commit v6 on v5

--- a/solution.py
+++ b/solution.py
@@ -450,13 +450,18 @@
                 probability = jnp.exp(scores_of(seq, 1, head) - log_sum[1, head])
                 probs[1, head] = probability.astype(BF16)
             d_weights = dot(qkv[which, head_rows(2, head)], d_out, 0, 0)
-            mean = jnp.sum(probability * d_weights, axis=0, keepdims=True)
+            if which == 0:
+                context = jnp.concatenate([ctx_out[0, 0, rows], ctx_out[0, 1, rows]], axis=1)
+                products = d_out.astype(F32) * context.astype(F32)
+            else:
+                products = probability * d_weights
+            mean = jnp.sum(products, axis=0, keepdims=True)
             d_scores.append((probability * (d_weights - mean)).astype(BF16))
         for head in range(3):
             rows = head_rows(0, head)
             d_out = jnp.concatenate([dctx_in[0, which, rows], dctx_in[1, which, rows]], axis=1)
-            d_query = (0.125 * dot(qkv[which, head_rows(1, head)], d_scores[head])).astype(BF16)
-            d_key = 0.125 * dot(d_scores[head], qkv[which, head_rows(0, head)], 1, 1)
+            d_query = dot(qkv[which, head_rows(1, head)] * jnp.asarray(0.125, BF16), d_scores[head]).astype(BF16)
+            d_key = dot(d_scores[head], qkv[which, head_rows(0, head)] * jnp.asarray(0.125, BF16), 1, 1)
             d_value = dot(probs[which, head], d_out, 1, 1)
             pieces = (d_query, d_key.astype(BF16).T, d_value.astype(BF16).T)
             for j, piece in enumerate(pieces):

time: 61.1 us -> 61.1 us (level)
  no operation moved by 1% of the time
where the time goes in v6:
time: 61.1 us; the launch traced here: 60.9 us
  Pallas kernels  60.1 us (98%)
  between operations  0.81 us (1%)
    pallas_call x1, Pallas kernels, body(): pl.pallas_call(functools.partial(kernel, batch), out_shape=(vmem((4, 256,...  58.4 us
    pallas_call x1, Pallas kernels, body(): pl.pallas_call(hand_over, out_shape=(rows, rows, small, small), in_specs=...  1.7 us

profile of v6, /device:TPU:0, one launch (start us, length us, event | category | flops | bytes accessed | tf_op | source)
XLA Modules:
  0.0 60.9 jit_solution(17660509829085547983)
XLA Ops:
  0.6 58.4 %shard_map.174 = (bf16[4,256,768]{2,1,0:T(8,128)(2,1)S(1)}, bf16[4,256,768]{2,1,0:T(8,128)(2,1)S(1)}, f32[2,8,192]{2,1,0:T(8,128)S(1)}) custom-call(s32[2]{0:T(128)} %lengths.1, bf16[4,256,768]{2,1,0:T(8,128)(2,1)} %bitcast.12, bf16[192,768]{1,0:T(8,128)(2,1)} %bitcast.18, bf16[192,768]{1,0:T(8,128)(2,1)} %bitcast.19, bf16[192,768]{1,0:T(8,128)(2,1)} %bitcast.20, ...), custom_call_target="tpu_custom_call" | custom-call | flops 11000000512 | bytes 20000000 | tf_op jit(solution)/shard_map/pallas_call | solution.py:619
  59.1 1.7 %shard_map.175 = (bf16[4,256,768]{2,1,0:T(8,128)(2,1)}, bf16[4,256,768]{2,1,0:T(8,128)(2,1)}, f32[8,192]{1,0:T(8,128)}, f32[8,192]{1,0:T(8,128)}) custom-call(bf16[4,256,768]{2,1,0:T(8,128)(2,1)S(1)} %get-tuple-element.11.activations, bf16[4,256,768]{2,1,0:T(8,128)(2,1)S(1)} %get-tuple-element.12.input_grad, f32[2,8,192]{2,1,0:T(8,128)S(1)} %get-tuple-element.13.grads), custom_call_target="tpu_custom_call" | custom-call | tf_op jit(solution)/shard_map/pallas_call | solution.py:690

commit v7 on v5

--- a/solution.py
+++ b/solution.py
@@ -425,19 +425,17 @@
     d_z1_low = d_z1.astype(BF16)
     relay(11)
 
-    def d_context(first):
-        pair = [w[first, OUT], w[first + 2, OUT]]
-        d_ctx = dot(jnp.concatenate(pair, axis=0), d_z1_low, 1, 1).astype(BF16)
-        dctx_out[first] = d_ctx[:192]
-        dctx_out[first + 2] = d_ctx[192:]
-
-    d_context(SIB)
+    dctx_out[SIB] = dot(w[SIB, OUT], d_z1_low, 1, 1).astype(BF16)
     send("dctx", "dctx", dctx_out.at[SIB], dctx_in.at[core, 0], sibling)
-    send("dctx", "dctx", dctx_out.at[FARSIB], dctx_in.at[core, 1], sibling)
-    d_context(OWN)
+    rest = jnp.concatenate([w[FARSIB, OUT], w[OWN, OUT], w[FAR, OUT]], axis=0)
+    d_ctx = dot(rest, d_z1_low, 1, 1).astype(BF16)
+    dctx_out[FARSIB] = d_ctx[:192]
+    send("dctx", "far dctx", dctx_out.at[FARSIB], dctx_in.at[core, 1], sibling)
+    dctx_out[OWN] = d_ctx[192:384]
+    dctx_out[FAR] = d_ctx[384:]
     dctx_in[core, 0] = dctx_out[OWN]
     dctx_in[core, 1] = dctx_out[FAR]
-    arrived("dctx", dctx_in.at[1 - core])
+    arrived("dctx", dctx_in.at[1 - core, 0])
 
     def attend_back(which):
         d_scores = []
@@ -491,6 +489,7 @@
     arrived("b", ups_out.at[1])
     spread_up(1)
     arrived("l", log_sum.at[1])
+    arrived("far dctx", dctx_in.at[1 - core, 1])
     project(seq, 1, FAR, False)
     attend_back(1)
     adapter_rows(1)
@@ -655,7 +654,7 @@
             vmem((2 * batch.bit_length(), 2, 8, 192), F32),
             pltpu.SemaphoreType.DMA((9,)),
             pltpu.SemaphoreType.DMA((len(SEND_GROUPS),)),
-            pltpu.SemaphoreType.DMA((33 + 2 * len(TWICE) + batch.bit_length() + len(SPANS) + len(PIECES),)),
+            pltpu.SemaphoreType.DMA((34 + 2 * len(TWICE) + batch.bit_length() + len(SPANS) + len(PIECES),)),
         ],
         compiler_params=pltpu.CompilerParams(
             collective_id=0, has_side_effects=True, vmem_limit_bytes=56 * 1024 * 1024

time: 61.1 us -> 61.1 us (level)
  no operation moved by 1% of the time
where the time goes in v7:
time: 61.1 us; the launch traced here: 61 us
  Pallas kernels  60.2 us (99%)
  between operations  0.81 us (1%)
    pallas_call x1, Pallas kernels, body(): pl.pallas_call(functools.partial(kernel, batch), out_shape=(vmem((4, 256,...  58.5 us
    pallas_call x1, Pallas kernels, body(): pl.pallas_call(hand_over, out_shape=(rows, rows, small, small), in_specs=...  1.7 us

profile of v7, /device:TPU:0, one launch (start us, length us, event | category | flops | bytes accessed | tf_op | source)
XLA Modules:
  0.0 61.0 jit_solution(6912380515324851978)
XLA Ops:
  0.6 58.5 %shard_map.174 = (bf16[4,256,768]{2,1,0:T(8,128)(2,1)S(1)}, bf16[4,256,768]{2,1,0:T(8,128)(2,1)S(1)}, f32[2,8,192]{2,1,0:T(8,128)S(1)}) custom-call(s32[2]{0:T(128)} %lengths.1, bf16[4,256,768]{2,1,0:T(8,128)(2,1)} %bitcast.12, bf16[192,768]{1,0:T(8,128)(2,1)} %bitcast.18, bf16[192,768]{1,0:T(8,128)(2,1)} %bitcast.19, bf16[192,768]{1,0:T(8,128)(2,1)} %bitcast.20, ...), custom_call_target="tpu_custom_call" | custom-call | flops 11000000512 | bytes 20000000 | tf_op jit(solution)/shard_map/pallas_call | solution.py:613
  59.1 1.7 %shard_map.175 = (bf16[4,256,768]{2,1,0:T(8,128)(2,1)}, bf16[4,256,768]{2,1,0:T(8,128)(2,1)}, f32[8,192]{1,0:T(8,128)}, f32[8,192]{1,0:T(8,128)}) custom-call(bf16[4,256,768]{2,1,0:T(8,128)(2,1)S(1)} %get-tuple-element.11.activations, bf16[4,256,768]{2,1,0:T(8,128)(2,1)S(1)} %get-tuple-element.12.input_grad, f32[2,8,192]{2,1,0:T(8,128)S(1)} %get-tuple-element.13.grads), custom_call_target="tpu_custom_call" | custom-call | tf_op jit(solution)/shard_map/pallas_call | solution.py:684
